TPU v7x, 32 devices: a whole 2x2x4 slice. The times are simulated.
32 devices in a mesh: dp: 8 (over z, y), mp: 4 (over x, core).
Axes of the slice: x: 2, y: 2, z: 4, core: 2. Of those that a mesh axis runs over, the one named last changes fastest.
Arguments:
- patches: bfloat16 [40, 198, 384], P('dp'), may hold values from -6 to 6
- targets: bfloat16 [40, 198, 384], P('dp'), may hold values from -6 to 6
- keep_mask: int32 [40, 196], P('dp'), may hold values from 0 to 1
- attn_weights: bfloat16 [2, 384, 1536], P(None, None, ('dp', 'mp')), may hold values from -0.8164966 to 0.8164966
- vectors: bfloat16 [2, 4608], P(None, ('dp', 'mp')), may hold values from -1.2 to 1.8
- up_weights: bfloat16 [2, 384, 1536], P(None, 'dp', 'mp'), may hold values from -0.3125 to 0.3125
- down_weights: bfloat16 [2, 1536, 384], P(None, 'mp', 'dp'), may hold values from -0.15625 to 0.15625
Outputs:
- activations: float32 [8192, 384], P('dp')
- input_grads: float32 [40, 198, 384], P('dp')
- attn_grads: float32 [2, 384, 1536], P(None, None, ('dp', 'mp'))
- vector_grads: float32 [2, 4608], P(None, ('dp', 'mp'))
- up_grads: float32 [2, 384, 1536], P(None, 'dp', 'mp')
- down_grads: float32 [2, 1536, 384], P(None, 'mp', 'dp')
All inputs are finite; a program needn't handle non-finite values.
Results may differ from a plain program's by a relative error of at most 0.013.
Values may be sent and summed in bfloat16 or wider, within the bound.
No kernel may reach another device: no remote copies, remote signals or barrier semaphores. Data moves between devices by JAX's collectives and lax.ppermute only.
A program may use at most 128 MiB of HBM per device.

v0:
```python
import dataclasses
import functools

import jax
import jax.numpy as jnp
from jax import lax
from jax.experimental import pallas as pl
from jax.experimental.pallas import tpu as pltpu
from jax.sharding import PartitionSpec as P

HD = 64
SLOTS = 1024
EPSILON = 1e-06
MASKED = -1e30
STEP = 16

F32 = jnp.float32
BF16 = jnp.bfloat16


def dot_nn(left, right):
    return lax.dot_general(left, right, (((1,), (0,)), ((), ())), preferred_element_type=F32)


def dot_nt(left, right):
    return lax.dot_general(left, right, (((1,), (1,)), ((), ())), preferred_element_type=F32)


def dot_tn(left, right):
    return lax.dot_general(left, right, (((0,), (0,)), ((), ())), preferred_element_type=F32)


def block_rows(index, step):
    return pl.ds(pl.multiple_of(index * step, step), step)


def fold_rows(values):
    return jnp.sum(values.reshape(values.shape[0] // 8, 8, values.shape[1]), axis=0)


def low_halves(rows):
    lane = lax.broadcasted_iota(jnp.int32, (rows, 2 * HD), 1)
    return lane < HD


def stack_heads(pair):
    low = low_halves(pair.shape[0])
    zero = jnp.zeros_like(pair)
    return jnp.concatenate([jnp.where(low, pair, zero), jnp.where(low, zero, pair)], axis=0)


def unstack_heads(stacked):
    rows = stacked.shape[0] // 2
    return jnp.where(low_halves(rows), stacked[:rows], stacked[rows:])


def norm_rows(x_ref, out_ref, gain, shift):
    def body(index, carry):
        at = block_rows(index, STEP)
        values = x_ref[at, :].astype(F32)
        centred = values - jnp.mean(values, axis=-1, keepdims=True)
        variance = jnp.mean(centred * centred, axis=-1, keepdims=True)
        out_ref[at, :] = (centred * lax.rsqrt(variance + EPSILON) * gain + shift).astype(BF16)
        return carry

    lax.fori_loop(0, x_ref.shape[0] // STEP, body, 0, unroll=True)


def norm_back(x_ref, grad_ref, base_ref, out_ref, low_ref, gain, images):
    rows = x_ref.shape[0] // images
    width = x_ref.shape[1]
    sums = []
    for image in range(images):

        def body(index, carry, image=image):
            at = pl.ds(pl.multiple_of(image * rows + index * STEP, STEP), STEP)
            values = x_ref[at, :].astype(F32)
            grad = grad_ref[at, :]
            centred = values - jnp.mean(values, axis=-1, keepdims=True)
            variance = jnp.mean(centred * centred, axis=-1, keepdims=True)
            inverse = lax.rsqrt(variance + EPSILON)
            unit = centred * inverse
            scaled = grad * gain
            mean_one = jnp.mean(scaled, axis=-1, keepdims=True)
            mean_two = jnp.mean(scaled * unit, axis=-1, keepdims=True)
            out = base_ref[at, :] + inverse * (scaled - mean_one - unit * mean_two)
            out_ref[at, :] = out.astype(out_ref.dtype)
            if low_ref is not None:
                low_ref[at, :] = out.astype(BF16)
            return (
                carry[0] + fold_rows(grad * unit),
                carry[1] + fold_rows(grad),
                carry[2] + fold_rows(out),
            )

        zero = jnp.zeros((8, width), F32)
        sums.append(lax.fori_loop(0, rows // STEP, body, (zero, zero, zero), unroll=True))
    return sums


def weigh(sums, share):
    total = sums[0]
    for more in sums[1:]:
        total = total + more * share
    return jnp.sum(total, axis=0, keepdims=True)


def as_square(ref, part):
    rows, width = ref.shape[1:]
    per = width // rows
    return ref[pl.ds(part * per, per)].reshape(width, width)


def forward_attention(x_ref, bias_ref, vec_ref, attn_ref, keep, mid_ref):
    n1_ref, proj_ref, p_ref, att_ref = keep
    images = bias_ref.shape[0]
    rows = x_ref.shape[0] // images
    width = x_ref.shape[1]
    pairs = width // (2 * HD)
    scale = HD**-0.5

    norm_rows(x_ref, n1_ref, vec_ref[0:1, :], vec_ref[1:2, :])
    for part, bias_row in enumerate((4, None, 5)):
        value = dot_nt(n1_ref[...], as_square(attn_ref, part))
        if bias_row is not None:
            value = value + vec_ref[bias_row : bias_row + 1, :]
        proj_ref[part] = value.astype(BF16)

    def image_body(image, carry):
        at = block_rows(image, rows)
        for pair in range(pairs):
            lanes = slice(pair * 2 * HD, (pair + 1) * 2 * HD)
            query = stack_heads(proj_ref[0, at, lanes])
            scores = dot_nt(query, proj_ref[1, at, lanes]) * scale + bias_ref[image]
            top = jnp.max(scores, axis=-1, keepdims=True)
            powers = jnp.exp(scores - top)
            total = jnp.sum(powers, axis=-1, keepdims=True)
            probs = (powers * (1.0 / total)).astype(BF16)
            p_ref[image, pair] = probs
            att_ref[at, lanes] = unstack_heads(dot_nn(probs, proj_ref[2, at, lanes])).astype(BF16)
        return carry

    for image in range(images):
        image_body(image, 0)
    mid_ref[...] = x_ref[...].astype(F32) + dot_nt(att_ref[...], as_square(attn_ref, 3)) + vec_ref[6:7, :]


def forward_hidden(mid_ref, vec_ref, up_ref, down_ref, keep, scratch, out_ref):
    n2_ref, a_ref, gp_ref = keep
    h_ref, acc_ref = scratch
    norm_rows(mid_ref, n2_ref, vec_ref[2:3, :], vec_ref[3:4, :])
    acc_ref[...] = mid_ref[...] + vec_ref[11:12, :]

    def part_body(part, carry):
        h_ref[part % 2] = dot_nn(n2_ref[...], as_square(up_ref, part))
        bias = vec_ref[pl.ds(7 + part, 1), :]

        def gelu_body(index, inner):
            at = block_rows(index, STEP)
            hidden = h_ref[part % 2, at, :] + bias
            share = 0.5 + 0.5 * lax.erf(hidden * 0.7071067811865476)
            a_ref[part, at, :] = (hidden * share).astype(BF16)
            bell = jnp.exp(-0.5 * hidden * hidden) * 0.3989422804014327
            gp_ref[part, at, :] = (share + hidden * bell).astype(gp_ref.dtype)
            return inner

        lax.fori_loop(0, h_ref.shape[1] // STEP, gelu_body, 0, unroll=True)
        acc_ref[...] += dot_nt(a_ref[part], as_square(down_ref, part))
        return carry

    for part in range(a_ref.shape[0]):
        part_body(part, 0)
    out_ref[...] = acc_ref[...].astype(out_ref.dtype)


def drop_shared(refs):
    @pl.when(jnp.logical_not(counts_shared()))
    def _():
        for ref in refs:
            rows = ref.shape[-2] // 2
            ref[..., rows:, :] = jnp.zeros((*ref.shape[:-2], rows, ref.shape[-1]), ref.dtype)


def backward_hidden(g_ref, mid_ref, vec_ref, up_ref, down_ref, share, keep, scratch, gm_ref, gvec_ref, store):
    n2_ref, a_ref, gp_ref = keep
    go_ref, gh_ref, acc_ref, h_ref, got_ref, n2t_ref = scratch
    images = 2
    rows = mid_ref.shape[0] // images
    width = mid_ref.shape[1]
    zero = jnp.zeros((8, width), F32)
    sums = []
    for image in range(images):

        def low_body(index, carry, image=image):
            at = pl.ds(pl.multiple_of(image * rows + index * STEP, STEP), STEP)
            grad = g_ref[at, :]
            go_ref[at, :] = grad.astype(BF16)
            return carry + fold_rows(grad)

        sums.append(lax.fori_loop(0, rows // STEP, low_body, zero, unroll=True))
    gvec_ref[11:12, :] = weigh(sums, share)
    acc_ref[...] = jnp.zeros_like(acc_ref)
    got_ref[...] = go_ref[...].T
    n2t_ref[...] = n2_ref[...].T

    def part_body(part, carry):
        store(2, part, dot_nn(got_ref[...], a_ref[part]))
        h_ref[part % 2] = dot_nn(go_ref[...], as_square(down_ref, part))
        inner_sums = []
        for image in range(images):

            def hidden_body(index, inner, image=image):
                at = pl.ds(pl.multiple_of(image * rows + index * STEP, STEP), STEP)
                grad = (h_ref[part % 2, at, :] * gp_ref[part, at, :].astype(F32)).astype(BF16)
                gh_ref[part % 2, at, :] = grad
                return inner + fold_rows(grad.astype(F32))

            inner_sums.append(lax.fori_loop(0, rows // STEP, hidden_body, zero, unroll=True))
        gvec_ref[pl.ds(7 + part, 1), :] = weigh(inner_sums, share)
        store(1, part, dot_nn(n2t_ref[...], gh_ref[part % 2]))
        acc_ref[...] += dot_nt(gh_ref[part % 2], as_square(up_ref, part))
        return carry

    for part in range(a_ref.shape[0]):
        part_body(part, 0)
    sums = norm_back(mid_ref, acc_ref, g_ref, gm_ref, None, vec_ref[2:3, :], images)
    for place, row in enumerate((2, 3, 6)):
        gvec_ref[row : row + 1, :] = weigh([one[place] for one in sums], share)


def backward_attention(gm_ref, x_ref, vec_ref, attn_ref, share, keep, scratch, gx_ref, gvec_ref, store):
    n1_ref, proj_ref, p_ref, att_ref = keep
    go_ref, acc_ref, ga_ref, dproj_ref = scratch
    images = p_ref.shape[0]
    rows = x_ref.shape[0] // images
    width = x_ref.shape[1]
    pairs = width // (2 * HD)
    scale = HD**-0.5
    go_ref[...] = gm_ref[...].astype(BF16)
    store(0, 3, dot_tn(go_ref[...], att_ref[...]))
    ga_ref[...] = dot_nn(go_ref[...], as_square(attn_ref, 3)).astype(BF16)

    def image_body(image, carry):
        at = block_rows(image, rows)
        for pair in range(pairs):
            lanes = slice(pair * 2 * HD, (pair + 1) * 2 * HD)
            query = stack_heads(proj_ref[0, at, lanes])
            keys = proj_ref[1, at, lanes]
            grad_out = stack_heads(ga_ref[at, lanes])
            probs = p_ref[image, pair]
            grad_probs = dot_nt(grad_out, proj_ref[2, at, lanes])
            dproj_ref[2, at, lanes] = dot_tn(probs, grad_out).astype(BF16)
            wide = probs.astype(F32)
            inner = jnp.sum(grad_probs * wide, axis=-1, keepdims=True)
            grad_scores = (wide * (grad_probs - inner)).astype(BF16)
            dproj_ref[0, at, lanes] = (unstack_heads(dot_nn(grad_scores, keys)) * scale).astype(BF16)
            dproj_ref[1, at, lanes] = (dot_tn(grad_scores, query) * scale).astype(BF16)
        return carry

    for image in range(images):
        image_body(image, 0)
    for part, row in enumerate((4, None, 5)):
        store(0, part, dot_tn(dproj_ref[part], n1_ref[...]))
        value = dot_nn(dproj_ref[part], as_square(attn_ref, part))
        if part == 0:
            acc_ref[...] = value
        else:
            acc_ref[...] += value
        if row is not None:
            sums = [
                fold_rows(dproj_ref[part, image * rows : (image + 1) * rows, :].astype(F32))
                for image in range(images)
            ]
            gvec_ref[row : row + 1, :] = weigh(sums, share)
    sums = norm_back(x_ref, acc_ref, gm_ref, gx_ref, None, vec_ref[0:1, :], images)
    for place, row in enumerate((0, 1)):
        gvec_ref[row : row + 1, :] = weigh([one[place] for one in sums], share)
    store(3, 0, gvec_ref[...])


def coordinates(plan):
    outer, inner = lax.axis_index("dp"), lax.axis_index("mp")
    here = (inner // 2, inner % 2)
    return (outer // 2, outer % 2, *here) if plan.direct else (0, 0, *here)


def counts_shared():
    return lax.axis_index("mp") == 0


def place_weights(plan, pieces, attn_ref, up_ref, down_ref, vec_ref):
    thin, rows = plan.thin, 3 * plan.thin

    def put(owner, block):
        at = owner % plan.inner * plan.outer + owner // plan.inner
        attn_ref[owner] = block[:thin]
        up_ref[at] = block[thin : 2 * thin]
        down_ref[at] = block[2 * thin : 3 * thin]

    if not plan.direct:
        for owner in range(plan.inner):
            put(owner, pieces[0][owner, :rows])
        vec_ref[...] = pieces[0][0, rows:].astype(F32)
        return
    at = coordinates(plan)
    vec = None
    for i, piece in enumerate(pieces):
        c, x, y = i % 2, i // 2 % 2, i // 4
        low = ((at[1] ^ y) * 2 + (at[2] ^ x)) * 2 + (at[3] ^ c)
        count = piece.shape[0] // rows
        for k in range(count):
            put((at[0] ^ k) * 8 + low, piece[k * rows : (k + 1) * rows])
        tail = piece[count * rows :].astype(F32)
        vec = tail if vec is None else vec + tail
    vec_ref[...] = vec


def storer(plan, packed_ref, kinds):
    thin, width = plan.thin, plan.width
    per = width // thin
    here = coordinates(plan)

    def put(owner, kind, block):
        c, x, y = owner % 2, owner // 2 % 2, owner // 4 % 2
        row = pl.multiple_of((kinds.index(kind) * plan.zs + owner // 8) * thin, thin)
        packed_ref[c ^ here[3], y ^ here[1], x ^ here[2], pl.ds(row, thin), :] = block

    def store(kind, part, value):
        low = value.astype(BF16)
        if kind == 3:
            for i in range(8):
                packed_ref[i % 2, i // 4, i // 2 % 2, len(kinds) * plan.zs * thin :, :] = low
            return
        blocks = low.reshape(per, thin, width)
        for i in range(per):
            owner = part * per + i if kind == 0 else i * plan.inner + part
            put(owner, kind, blocks[i])

    return store


def start_copies(packed_ref, outs, sems, start, count, before=()):
    at = pl.ds(start, count)
    copies = list(before)
    for i in range(2):
        source, target = packed_ref.at[i, :, :, at], outs[i].at[:, :, at]
        copies.append(pltpu.make_async_copy(source, target, sems.at[len(copies)]))
        copies[-1].start()
    return copies


def wait_all(copies):
    for one in copies:
        one.wait()


def prepare_kernel(plan, attn_ref, up_ref, down_ref, vec_in, keep_in, first_ref, last_ref, line_ref, vec_ref, keep_ref, sems):
    thin, tile, width = plan.thin, plan.tile, plan.width
    outs = (first_ref, last_ref)
    copies = [
        pltpu.make_async_copy(vec_in, vec_ref, sems.at[0]),
        pltpu.make_async_copy(keep_in, keep_ref, sems.at[1]),
    ]
    for kind, ref in enumerate((attn_ref, up_ref, down_ref)):
        for layer, out_ref in enumerate(outs):
            if plan.direct:
                target = out_ref.at[pl.ds(kind * thin, thin)]
                copies.append(pltpu.make_async_copy(ref.at[layer], target, sems.at[len(copies)]))
            else:
                out_ref[kind * thin : (kind + 1) * thin, :] = ref[layer]
    for one in copies:
        one.start()
    count = vec_ref.shape[1]
    device = lax.axis_index("dp") * plan.inner + lax.axis_index("mp")
    row_at = device * count // width
    offset = device * count - row_at * width
    copies[0].wait()
    copies[1].wait()
    kept = jnp.sum(keep_ref[...]) + 2 * keep_ref.shape[0]
    kept = jnp.where(counts_shared(), kept, 0)
    row = lax.broadcasted_iota(jnp.int32, (tile, width), 0)
    here = lax.broadcasted_iota(jnp.int32, (tile, width), 1) == lax.axis_index("dp")
    for layer, out_ref in enumerate(outs):
        line_ref[...] = jnp.zeros_like(line_ref)
        line_ref[0:1, 0:count] = vec_ref[layer : layer + 1, :].astype(F32)
        moved = pltpu.roll(line_ref[...], offset, 1)[0:1]
        piece = jnp.where(row == row_at, moved[:, :width], 0.0)
        piece = jnp.where(row == row_at + 1, moved[:, width:], piece)
        if layer == 1:
            piece = jnp.where(here & (row == 12), (kept >> 5).astype(F32), piece)
            piece = jnp.where(here & (row == 13), (kept & 31).astype(F32), piece)
        out_ref[3 * thin :, :] = piece.astype(BF16)
    for one in copies[2:]:
        one.wait()


def forward_kernel(plan, pieces, x_ref, bias_ref, *refs):
    sources, refs = refs[:pieces], refs[pieces:]
    attn_ref, up_ref, down_ref, vec_ref, mid_ref, out_ref, *refs = refs
    attn_keep, hidden_keep, (h_ref, acc_ref) = refs[:4], refs[4:7], refs[7:]
    place_weights(plan, sources, attn_ref, up_ref, down_ref, vec_ref)
    forward_attention(x_ref, bias_ref, vec_ref, attn_ref, attn_keep, mid_ref)
    forward_hidden(mid_ref, vec_ref, up_ref, down_ref, hidden_keep, (h_ref, acc_ref), out_ref)
    drop_shared((attn_keep[0], attn_keep[3], hidden_keep[0], hidden_keep[1]))


HIDDEN_KINDS, ATTENTION_KINDS, ALL_KINDS = (1, 2), (0,), (1, 2, 0)


def last_hidden_kernel(plan, goal_ref, mid_ref, vec_ref, up_ref, down_ref, *refs):
    keep, gm_ref, gvec_ref, outs, refs = refs[:3], refs[3], refs[4], refs[5:7], refs[7:]
    g_ref, go_ref, gh_ref, acc_ref, h_ref, got_ref, n2t_ref, packed_ref, sems = refs
    high = jnp.sum(vec_ref[12:13, :], axis=-1, keepdims=True)
    rest = jnp.sum(vec_ref[13:14, :], axis=-1, keepdims=True)
    loss_scale = float(plan.slots) / (high * 32.0 + rest)
    g_ref[...] = goal_ref[...].astype(F32) * loss_scale
    gvec_ref[...] = jnp.zeros_like(gvec_ref)
    share = counts_shared().astype(F32)
    store = storer(plan, packed_ref, HIDDEN_KINDS)
    scratch = (go_ref, gh_ref, acc_ref, h_ref, got_ref, n2t_ref)
    backward_hidden(g_ref, mid_ref, vec_ref, up_ref, down_ref, share, keep, scratch, gm_ref, gvec_ref, store)
    wait_all(start_copies(packed_ref, outs, sems, 0, packed_ref.shape[3]))


def last_attention_kernel(plan, gm_ref, x_ref, vec_ref, attn_ref, early_ref, *refs):
    keep, gx_ref, outs, refs = refs[:4], refs[4], refs[5:7], refs[7:]
    gvec_ref, go_ref, acc_ref, ga_ref, dproj_ref, packed_ref, sems = refs
    gvec_ref[...] = early_ref[...]
    share = counts_shared().astype(F32)
    store = storer(plan, packed_ref, ATTENTION_KINDS)
    scratch = (go_ref, acc_ref, ga_ref, dproj_ref)
    backward_attention(gm_ref, x_ref, vec_ref, attn_ref, share, keep, scratch, gx_ref, gvec_ref, store)
    wait_all(start_copies(packed_ref, outs, sems, 0, packed_ref.shape[3]))


def back_kernel(plan, g_ref, x_ref, mid_ref, vec_ref, attn_ref, up_ref, down_ref, *refs):
    attn_keep, hidden_keep, gx_ref, outs, refs = refs[:4], refs[4:7], refs[7], refs[8:10], refs[10:]
    gm_ref, gvec_ref, go_ref, gh_ref, ga_ref, acc_ref, h_ref, got_ref, n2t_ref, dproj_ref, packed_ref, sems = refs
    gvec_ref[...] = jnp.zeros_like(gvec_ref)
    share = counts_shared().astype(F32)
    store = storer(plan, packed_ref, ALL_KINDS)
    scratch = (go_ref, gh_ref, acc_ref, h_ref, got_ref, n2t_ref)
    backward_hidden(g_ref, mid_ref, vec_ref, up_ref, down_ref, share, hidden_keep, scratch, gm_ref, gvec_ref, store)
    hidden_rows = 2 * plan.zs * plan.thin
    copies = start_copies(packed_ref, outs, sems, 0, hidden_rows)
    scratch = (go_ref, acc_ref, ga_ref, dproj_ref)
    backward_attention(gm_ref, x_ref, vec_ref, attn_ref, share, attn_keep, scratch, gx_ref, gvec_ref, store)
    rest = packed_ref.shape[3] - hidden_rows
    wait_all(start_copies(packed_ref, outs, sems, hidden_rows, rest, copies))


def add_kernel(kept_hidden, got_hidden, kept_attn, got_attn, *out_refs):
    count = kept_hidden.shape[2]
    for i, out_ref in enumerate(out_refs):
        at = (i // 2, i % 2)
        total = kept_hidden[at].astype(F32) + got_hidden[at].astype(F32)
        out_ref[0:count, :] = total.astype(BF16)
        total = kept_attn[at].astype(F32) + got_attn[at].astype(F32)
        out_ref[count:, :] = total.astype(BF16)


def finish_kernel(plan, *refs):
    late, early = refs[0], refs[1 : 1 + plan.zs]
    attn_out, vec_out, up_out, down_out, *tiles = refs[1 + plan.zs :]
    thin, tile, width = plan.thin, plan.tile, plan.width

    count = vec_out.shape[1]
    device = lax.axis_index("dp") * plan.inner + lax.axis_index("mp")
    row = device * count // width
    offset = device * count - row * width
    for layer in range(2):

        def total(start, count, layer=layer):
            at = slice(start, start + count)
            blocks = [early[k][at, :] if layer == 0 else late[k, at, :] for k in range(plan.zs)]
            return sum(block.astype(F32) for block in blocks)

        attn_out[layer] = total(0, thin)
        up_out[layer] = total(thin, thin)
        down_out[layer] = total(2 * thin, thin)
        tiles[layer][...] = total(3 * thin, tile)
        both = jnp.concatenate(
            [tiles[layer][pl.ds(row, 1), :], tiles[layer][pl.ds(row + 1, 1), :]], axis=1
        )
        both = jnp.broadcast_to(both, (8, 2 * width))
        moved = pltpu.roll(both, 2 * width - offset, 1)
        vec_out[layer : layer + 1, :] = moved[0:1, :count]


def place_kernel(own_ref, *refs):
    others, out_ref = refs[:-1], refs[-1]
    rows = own_ref.shape[0] // 2
    kept = out_ref.shape[1]
    mine = lax.axis_index("mp")
    out_ref[mine] = own_ref[0:rows, :].astype(F32)[:kept]
    for i, ref in enumerate(others):
        out_ref[mine ^ (i + 1)] = ref[...].astype(F32)[:kept]
    out_ref[out_ref.shape[0] - 1] = own_ref[rows : 2 * rows, :].astype(F32)[:kept]


def pack_kernel(slot_ref, own_ref, *refs):
    others, out_ref = refs[:-1], refs[-1]
    rows = own_ref.shape[0] // 2
    sources = [own_ref[0:rows, :]] + [ref[...] for ref in others] + [own_ref[rows : 2 * rows, :]]
    step = 256

    def body(index, carry):
        slots = lax.broadcasted_iota(jnp.int32, (step, rows), 0) + index * step
        total = None
        for i, values in enumerate(sources):
            picks = jnp.where(slots == slot_ref[i], 1.0, 0.0).astype(BF16)
            term = dot_nn(picks, values)
            total = term if total is None else total + term
        out_ref[block_rows(index, step), :] = total
        return carry

    lax.fori_loop(0, out_ref.shape[0] // step, body, 0)


VMEM = pl.BlockSpec(memory_space=pltpu.VMEM)
ANY = pl.BlockSpec(memory_space=pl.ANY)


def call(kernel, operands, specs, outs, out_specs, scratch, flops, limit=26):
    return pl.pallas_call(
        kernel,
        out_shape=[jax.ShapeDtypeStruct(shape, dtype) for shape, dtype in outs],
        in_specs=specs,
        out_specs=out_specs,
        scratch_shapes=scratch,
        compiler_params=pltpu.CompilerParams(vmem_limit_bytes=limit << 20),
        cost_estimate=pl.CostEstimate(flops=flops, bytes_accessed=8 << 20, transcendentals=0),
    )(*operands)


@dataclasses.dataclass(frozen=True)
class Plan:
    outer: int
    inner: int
    thin: int
    tile: int
    width: int
    slots: int
    direct: bool

    @property
    def zs(self):
        return self.outer // 2 if self.direct else 1


def flip(array, mask, devices):
    return lax.ppermute(array, ("dp", "mp"), [(d, d ^ mask) for d in range(devices)])


def column_kernel(plan, *refs):
    blocks, out_ref = refs[:-1], refs[-1]
    rows = 3 * plan.thin
    for k, ref in enumerate(blocks):
        out_ref[k * rows : (k + 1) * rows, :] = ref[0:rows, :]
    tail = sum(ref[rows:, :].astype(F32) for ref in blocks)
    out_ref[len(blocks) * rows :, :] = tail.astype(BF16)


def gather_column(plan, block, devices):
    blocks = [block] + [flip(block, 8 * k, devices) for k in range(1, devices // 8)]
    shape = (len(blocks) * 3 * plan.thin + plan.tile, plan.width)
    (column,) = call(
        functools.partial(column_kernel, plan), blocks, [VMEM] * len(blocks), [(shape, BF16)], [VMEM], [], 1 << 20
    )
    return column


def gather_plane(column, devices):
    return [column] + [flip(column, mask, devices) for mask in (2, 4, 6)]


def gather_cores(plane, devices):
    pieces = []
    for piece in plane:
        pieces += [piece, flip(piece, 1, devices)]
    return pieces


def spread(rows, devices):
    across = flip(rows, 2, devices)
    return [flip(rows, 1, devices), across, flip(across, 1, devices)]


def sum_cores(kept, sent, devices):
    got = flip(sent, 1, devices)
    return [(kept[i // 2, i % 2].astype(F32) + got[i // 2, i % 2].astype(F32)).astype(BF16) for i in range(4)]


def plane_kernel(plan, counts, *refs):
    terms, out_refs = [], refs[sum(counts) :]
    for k in range(len(counts)):
        start = sum(counts[:k])
        terms.append(refs[start : start + counts[k]])
    thin, tile = plan.thin, plan.tile
    zs, scratch = plan.zs, out_refs[-1]
    rows = scratch.shape[0]
    total = None
    for parts in terms:
        whole = jnp.concatenate([ref[...].astype(F32) for ref in parts], axis=0)
        total = whole if total is None else total + whole
    scratch[...] = total
    tail = scratch[rows - tile :, :].astype(BF16)
    one = len(out_refs) == 2
    for z in range(zs):
        for kind in range(3):
            at = z if one else coordinates(plan)[0] ^ z
            row = pl.multiple_of((ALL_KINDS.index(kind) * zs + at) * thin, thin)
            block = scratch[pl.ds(row, thin), :].astype(BF16)
            if one:
                out_refs[0][z, kind * thin : (kind + 1) * thin, :] = block
            else:
                out_refs[z][kind * thin : (kind + 1) * thin, :] = block
        if one:
            out_refs[0][z, 3 * thin :, :] = tail
        else:
            out_refs[z][3 * thin :, :] = tail


def sum_plane(plan, sums, devices, relayed):
    rows = sums[0].shape[0]
    if relayed:
        half = rows // 2 // 16 * 16
        own, x_sum, y_sum, both = sums
        x_first, y_first = flip(both[:half], 2, devices), flip(both[half:], 4, devices)

        def joined(one, two):
            return (one.astype(F32) + two.astype(F32)).astype(BF16)

        x_two, y_one = joined(x_sum[half:], y_first), joined(y_sum[:half], x_first)
        x_parts = [flip(x_sum[:half], 2, devices), flip(x_two, 2, devices)]
        y_parts = [flip(y_one, 4, devices), flip(y_sum[half:], 4, devices)]
        terms, counts = [own, *x_parts, *y_parts], (1, 2, 2)
    else:
        terms = [sums[0]] + [flip(one, mask, devices) for one, mask in zip(sums[1:], (2, 4, 6))]
        counts = (1, 1, 1, 1)
    shape = (3 * plan.thin + plan.tile, plan.width)
    outs = [(shape, BF16)] * plan.zs if relayed else [((plan.zs, *shape), BF16)]
    return call(
        functools.partial(plane_kernel, plan, counts),
        terms,
        [VMEM] * len(terms),
        outs,
        [VMEM] * len(outs),
        [pltpu.VMEM((rows, plan.width), F32)],
        1 << 20,
    )


def sum_column(blocks, devices):
    return [one if k == 0 else flip(one, 8 * k, devices) for k, one in enumerate(blocks)]


def shards(patches, targets, keep_mask, attn_weights, vectors, up_weights, down_weights):
    image_count, patch_rows, width = patches.shape
    layers = attn_weights.shape[0]
    dp_size, mp_size = lax.axis_size("dp"), lax.axis_size("mp")
    devices = dp_size * mp_size
    rank = lax.axis_index("mp")
    lane_rank = lax.axis_index("dp")
    device = lane_rank * mp_size + rank
    thin = attn_weights.shape[2]
    vec_rows = vectors.shape[1]
    parts = thin * devices // width
    assert image_count == mp_size + 1 and layers == 2 and parts == mp_size == 4
    direct = thin % 16 == 0
    images, tile = 2, 16
    rows = -(-patch_rows // 16) * 16
    total = images * rows

    keep_rows = jnp.concatenate([jnp.ones((image_count, 2), jnp.int32), keep_mask], axis=1)
    keep_rows = jnp.pad(keep_rows, ((0, 0), (0, rows - patch_rows)))

    attn_turned = attn_weights.transpose(0, 2, 1)
    down_turned = down_weights.transpose(0, 2, 1)
    packing = Plan(dp_size, mp_size, thin, tile, width, SLOTS * dp_size, direct)
    block_shape = ((3 * thin + tile, width), BF16)
    first_block, last_block = call(
        functools.partial(prepare_kernel, packing),
        (attn_turned, up_weights, down_turned, vectors, keep_mask),
        [ANY if direct else VMEM] * 3 + [ANY] * 2,
        [block_shape, block_shape],
        [VMEM, VMEM],
        [
            pltpu.VMEM((8, 2 * width), F32),
            pltpu.VMEM(vectors.shape, BF16),
            pltpu.VMEM(keep_mask.shape, jnp.int32),
            pltpu.SemaphoreType.DMA((8,)),
        ],
        1 << 20,
        60,
    )
    if direct:
        plan = packing
        first_column = gather_column(plan, first_block, devices)
        first_column, last_block = lax.optimization_barrier((first_column, last_block))
        first_plane = gather_plane(first_column, devices)
        last_column = gather_column(plan, last_block, devices)
        first_plane, last_column = lax.optimization_barrier((first_plane, last_column))
        first_pieces = gather_cores(first_plane, devices)
        last_plane = gather_plane(last_column, devices)
    else:
        plan = Plan(1, parts, width, tile, width, SLOTS * dp_size, False)

        def squares(array):
            return array.reshape(parts, width, width)

        def by_part(array):
            split = array.reshape(dp_size, mp_size, thin, width).transpose(1, 0, 2, 3)
            return squares(split)

        def one_tile(array):
            summed = jnp.sum(array.astype(F32), axis=0).astype(BF16)
            return jnp.pad(summed[None], ((0, parts - 1), (0, 0), (0, 0)))

        def normal(block):
            every = lax.all_gather(block, ("dp", "mp"))
            return jnp.concatenate(
                [
                    squares(every[:, :thin]),
                    by_part(every[:, thin : 2 * thin]),
                    by_part(every[:, 2 * thin : 3 * thin]),
                    one_tile(every[:, 3 * thin :]),
                ],
                axis=1,
            )

        first_pieces, last_pieces = [normal(first_block)], [normal(last_block)]

    flat = keep_rows.reshape(-1)
    slot = jnp.where(flat == 1, jnp.cumsum(flat) - flat, SLOTS).reshape(image_count, 1, rows)

    def mine(array):
        return jnp.concatenate(
            [lax.dynamic_slice_in_dim(array, rank, 1, 0), array[mp_size:]], axis=0
        )

    def padded(array):
        return jnp.pad(mine(array), ((0, 0), (0, rows - patch_rows), (0, 0)))

    kept = mine(keep_rows)
    stream = padded(patches).reshape(total, width)
    bias = jnp.where(kept == 1, 0.0, MASKED).astype(F32)[:, None, :]
    goal = jnp.where((kept == 1)[:, :, None], padded(targets), 0).reshape(total, width)
    slots = jnp.concatenate(
        [lax.dynamic_slice_in_dim(slot, rank ^ k, 1, 0) for k in range(mp_size)] + [slot[mp_size:]],
        axis=0,
    )

    stream, slots, goal = lax.optimization_barrier((stream, slots, goal))

    pairs = width // (2 * HD)
    stream_shape = ((total, width), F32)
    low_shape = ((total, width), BF16)
    pair_shape, low_pair_shape = ((2, total, width), F32), ((2, total, width), BF16)
    three_shape = ((3, total, width), BF16)
    turned_shape = ((width, total), BF16)
    vec_shape = ((tile, width), F32)
    attn_keep = [low_shape, three_shape, ((images, pairs, 2 * rows, rows), BF16), low_shape]
    hidden_keep = [low_shape, ((parts, total, width), BF16), ((parts, total, width), F32)]
    blocks = plan.outer * plan.inner
    weight_shape = ((blocks, plan.thin, width), BF16)
    zs = max(blocks // 8, 1)

    def vmem(shapes):
        return [pltpu.VMEM(shape, dtype) for shape, dtype in shapes]

    layer_flops = 8 * total * parts * width * width
    hidden_rows, attn_rows = 2 * plan.thin * zs, plan.thin * zs + tile

    def half(count):
        return ((2, 2, count, width), BF16)

    def both(count):
        return ((2, 2, 2, count, width), BF16)


    def forward(rows_in, pieces, out_shape):
        results = call(
            functools.partial(forward_kernel, plan, len(pieces)),
            (rows_in, bias, *pieces),
            [VMEM] * (2 + len(pieces)),
            [weight_shape, weight_shape, weight_shape, vec_shape, stream_shape, out_shape]
            + attn_keep
            + hidden_keep,
            [VMEM] * 13,
            vmem([pair_shape, stream_shape]),
            layer_flops,
        )
        return (*results[:6], results[6:10], results[10:])

    attn_full, up_full, down_full, vec, mid, middle, attn_kept, hidden_kept = forward(
        stream, first_pieces, stream_shape
    )
    if direct:
        middle, last_plane = lax.optimization_barrier((middle, last_plane))
        last_pieces = gather_cores(last_plane, devices)
    sems = [pltpu.SemaphoreType.DMA((4,))]
    last_attn, last_up, last_down, last_vec, last_mid, output, last_kept, last_hidden_kept = forward(
        middle, last_pieces, low_shape
    )
    last_mid_grad, last_gvec, *last_hidden = call(
        functools.partial(last_hidden_kernel, plan),
        (goal, last_mid, last_vec, last_up, last_down, *last_hidden_kept),
        [VMEM] * 8,
        [stream_shape, vec_shape, half(hidden_rows), half(hidden_rows)],
        [VMEM] * 2 + [ANY] * 2,
        vmem(
            [stream_shape, low_shape, low_pair_shape, stream_shape, pair_shape]
            + [turned_shape, turned_shape, both(hidden_rows)]
        )
        + sems,
        layer_flops,
    )
    across = flip(output[:rows], 2, devices)
    last_mid_grad, last_gvec, last_hidden, across, output = lax.optimization_barrier(
        (last_mid_grad, last_gvec, last_hidden, across, output)
    )
    grad_middle, *last_attention = call(
        functools.partial(last_attention_kernel, plan),
        (last_mid_grad, middle, last_vec, last_attn, last_gvec, *last_kept),
        [VMEM] * 9,
        [stream_shape, half(attn_rows), half(attn_rows)],
        [VMEM, ANY, ANY],
        vmem([vec_shape, low_shape, stream_shape, low_shape, three_shape, both(attn_rows)]) + sems,
        layer_flops,
    )
    output_pieces = [flip(output[:rows], 1, devices), across, flip(across, 1, devices)]
    if direct:
        terms = []
        for kept_half, sent_half in (last_hidden, last_attention):
            terms += [kept_half, flip(sent_half, 1, devices)]
        message = ((hidden_rows + attn_rows, width), BF16)
        last_sums = call(add_kernel, terms, [VMEM] * 4, [message] * 4, [VMEM] * 4, [], 1 << 20)
        grad_middle, last_sums, output_pieces = lax.optimization_barrier(
            (grad_middle, last_sums, output_pieces)
        )
    grad_first, *first_halves = call(
        functools.partial(back_kernel, plan),
        (grad_middle, stream, mid, vec, attn_full, up_full, down_full, *attn_kept, *hidden_kept),
        [VMEM] * 14,
        [low_shape, half(hidden_rows + attn_rows), half(hidden_rows + attn_rows)],
        [VMEM, ANY, ANY],
        vmem(
            [stream_shape, vec_shape, low_shape, low_pair_shape, low_shape, stream_shape, pair_shape]
            + [turned_shape, turned_shape, three_shape, both(hidden_rows + attn_rows)]
        )
        + sems,
        3 * layer_flops,
    )

    def pack_output(output, output_pieces):
        (activations,) = call(
            pack_kernel,
            (slots, output, *output_pieces),
            [VMEM] * (mp_size + 1),
            [((SLOTS, width), F32)],
            [VMEM],
            [],
            2 * SLOTS * image_count * rows * width,
        )
        return activations

    def place_grads(grad_first, grad_pieces):
        (input_grads,) = call(
            place_kernel,
            (grad_first, *grad_pieces),
            [VMEM] * mp_size,
            [((image_count, patch_rows, width), F32)],
            [VMEM],
            [],
            image_count * patch_rows * width,
        )
        return input_grads

    if direct:
        (last_total,) = sum_plane(plan, last_sums, devices, False)
        activations = pack_output(output, output_pieces)
        last_total, first_halves, grad_first, activations = lax.optimization_barrier(
            (last_total, first_halves, grad_first, activations)
        )
        last_terms = last_total
        if plan.zs > 1:
            columns = [[8 * z + at for z in range(plan.zs)] for at in range(8)]
            last_terms = lax.all_to_all(
                last_total, ("dp", "mp"), 0, 0, axis_index_groups=columns, tiled=True
            )
        across = flip(grad_first[:rows], 2, devices)
        first_sums = sum_cores(*first_halves, devices)
        first_total = sum_plane(plan, first_sums, devices, True)
        beside = flip(grad_first[:rows], 1, devices)
        input_grads = place_grads(grad_first, [beside, across, flip(across, 1, devices)])
        first_total, last_terms, input_grads = lax.optimization_barrier(
            (first_total, last_terms, input_grads)
        )
        first_terms = sum_column(first_total, devices)
        terms = (last_terms, *first_terms)
        turned = (layers, thin, width)
        attn_grads, vector_grads, up_grads, down_grads = call(
            functools.partial(finish_kernel, plan),
            terms,
            [VMEM] * len(terms),
            [(turned, F32), (vectors.shape, F32), (turned, F32), (turned, F32)],
            [VMEM] * 4,
            vmem([vec_shape, vec_shape]),
            1 << 20,
        )
        attn_grads, down_grads = attn_grads.transpose(0, 2, 1), down_grads.transpose(0, 2, 1)
    else:
        last_halves = [
            jnp.concatenate(halves, axis=2) for halves in zip(last_hidden, last_attention)
        ]

        def square_blocks(halves):
            stacked = jnp.stack(halves)[:, 0]
            stacked = jnp.stack([stacked[k % 2, k // 2] for k in range(parts)])
            return jnp.stack(
                [lax.dynamic_index_in_dim(stacked, rank ^ k, 0, False) for k in range(parts)]
            )

        def outputs_of(halves):
            def by_owner(array):
                split = array.reshape(mp_size, dp_size, thin, width).transpose(1, 0, 2, 3)
                return split.reshape(devices, thin, width)

            every = square_blocks(halves)
            pieces = [
                every[:, 2 * width : 3 * width].reshape(devices, thin, width),
                by_owner(every[:, :width]),
                by_owner(every[:, width : 2 * width]),
                jnp.broadcast_to(every[0, 3 * width :], (devices, tile, width)),
            ]
            owned = lax.psum_scatter(
                jnp.concatenate(pieces, axis=1), ("dp", "mp"), scatter_dimension=0, tiled=False
            ).astype(F32)
            own_vec = lax.dynamic_slice_in_dim(
                owned[3 * thin :].reshape(-1), device * vec_rows, vec_rows
            )
            return owned[:thin].T, own_vec, owned[thin : 2 * thin], owned[2 * thin : 3 * thin].T

        attn_grads, vector_grads, up_grads, down_grads = (
            jnp.stack([one, two]) for one, two in zip(outputs_of(first_halves), outputs_of(last_halves))
        )
        activations = pack_output(output, output_pieces)
        input_grads = place_grads(grad_first, spread(grad_first[:rows], devices))

    return (activations, input_grads, attn_grads, vector_grads, up_grads, down_grads)


def solution(mesh):
    in_specs = (
        P("dp", None, None),
        P("dp", None, None),
        P("dp", None),
        P(None, None, ("dp", "mp")),
        P(None, ("dp", "mp")),
        P(None, "dp", "mp"),
        P(None, "mp", "dp"),
    )
    out_specs = (
        P("dp", None),
        P("dp", None, None),
        P(None, None, ("dp", "mp")),
        P(None, ("dp", "mp")),
        P(None, "dp", "mp"),
        P(None, "mp", "dp"),
    )
    return jax.shard_map(shards, mesh=mesh, in_specs=in_specs, out_specs=out_specs, check_vma=False)
```

profile of v0, /device:TPU:0, one launch (start us, length us, event | category | flops | bytes accessed | tf_op | source)
XLA Modules:
  0.0 153.8 jit_solution(1775946126530835211)
XLA Ops:
  2.3 5.1 %collective-permute-start.2 = (bf16[160,384]{1,0:T(8,128)(2,1)}, bf16[160,384]{1,0:T(8,128)(2,1)S(1)}, u32[]{:S(2)}, u32[]{:S(2)}) collective-permute-start(bf16[160,384]{1,0:T(8,128)(2,1)} %get-tuple-element.98.refs_0_), channel_id=1, source_target_pairs={{0,24},{1,25},{2,26},{3,27},{4,28},{5,29},{6,30},{7,31},{8,16},{9,... | collective-permute-start | bytes 368648 | tf_op jit(solution)/shard_map/ppermute | solution.py:552
  11.9 6.1 %collective-permute-done.1.refs_2_ = bf16[160,384]{1,0:T(8,128)(2,1)S(1)} collective-permute-done((bf16[160,384]{1,0:T(8,128)(2,1)}, bf16[160,384]{1,0:T(8,128)(2,1)S(1)}, u32[]{:S(2)}, u32[]{:S(2)}) %collective-permute-start.1) | collective-permute-done | bytes 122912 | tf_op jit(solution)/shard_map/ppermute | solution.py:552
  18.1 2.5 %collective-permute-start.5 = (bf16[592,384]{1,0:T(8,128)(2,1)S(1)}, bf16[592,384]{1,0:T(8,128)(2,1)S(1)}, u32[]{:S(2)}, u32[]{:S(2)}) collective-permute-start(bf16[592,384]{1,0:T(8,128)(2,1)S(1)} %shard_map.119.refs_0_), channel_id=1, source_target_pairs={{0,6},{1,7},{2,4},{3,5},{4,2},{5,3},{6,0},{7,1},{8,14},{9,15},{10,... | collective-permute-start | bytes 1363976 | tf_op jit(solution)/shard_map/ppermute | solution.py:552
  21.6 2.5 %collective-permute-start.8 = (bf16[160,384]{1,0:T(8,128)(2,1)S(1)}, bf16[160,384]{1,0:T(8,128)(2,1)S(1)}, u32[]{:S(2)}, u32[]{:S(2)}) collective-permute-start(bf16[160,384]{1,0:T(8,128)(2,1)S(1)} %copy-done), channel_id=1, source_target_pairs={{0,24},{1,25},{2,26},{3,27},{4,28},{5,29},{6,30},{7,31},{8,16},{9,... | collective-permute-start | bytes 368648 | tf_op jit(solution)/shard_map/ppermute | solution.py:552
  24.2 4.2 %collective-permute-done.8.refs_3_ = bf16[160,384]{1,0:T(8,128)(2,1)S(1)} collective-permute-done((bf16[160,384]{1,0:T(8,128)(2,1)S(1)}, bf16[160,384]{1,0:T(8,128)(2,1)S(1)}, u32[]{:S(2)}, u32[]{:S(2)}) %collective-permute-start.8) | collective-permute-done | bytes 122912 | tf_op jit(solution)/shard_map/ppermute | solution.py:552
  28.4 4.3 %collective-permute-start.6 = (bf16[160,384]{1,0:T(8,128)(2,1)S(1)}, bf16[160,384]{1,0:T(8,128)(2,1)S(1)}, u32[]{:S(2)}, u32[]{:S(2)}) collective-permute-start(bf16[160,384]{1,0:T(8,128)(2,1)S(1)} %copy-done), channel_id=1, source_target_pairs={{0,8},{1,9},{2,10},{3,11},{4,12},{5,13},{6,14},{7,15},{8,0},{9,1},... | collective-permute-start | bytes 368648 | tf_op jit(solution)/shard_map/ppermute | solution.py:552
  33.5 2.0 %collective-permute-done.6.refs_1_ = bf16[160,384]{1,0:T(8,128)(2,1)S(1)} collective-permute-done((bf16[160,384]{1,0:T(8,128)(2,1)S(1)}, bf16[160,384]{1,0:T(8,128)(2,1)S(1)}, u32[]{:S(2)}, u32[]{:S(2)}) %collective-permute-start.6) | collective-permute-done | bytes 122912 | tf_op jit(solution)/shard_map/ppermute | solution.py:552
  35.6 4.6 %collective-permute-done.4.refs_4_ = bf16[592,384]{1,0:T(8,128)(2,1)S(1)} collective-permute-done((bf16[592,384]{1,0:T(8,128)(2,1)S(1)}, bf16[592,384]{1,0:T(8,128)(2,1)S(1)}, u32[]{:S(2)}, u32[]{:S(2)}) %collective-permute-start.4) | collective-permute-done | bytes 454688 | tf_op jit(solution)/shard_map/ppermute | solution.py:552
  45.2 5.9 %shard_map.121 = (bf16[32,48,384]{2,1,0:T(8,128)(2,1)S(1)}, bf16[32,48,384]{2,1,0:T(8,128)(2,1)S(1)}, bf16[32,48,384]{2,1,0:T(8,128)(2,1)S(1)}, f32[16,384]{1,0:...) custom-call(bf16[416,384]{1,0:T(8,128)(2,1)S(1)} %bitcast.52, ...), custom_call_target="tpu_custom_call" | custom-call | flops 1962934272 | bytes 8388608 | tf_op jit(solution)/shard_map/pallas_call | solution.py:525
  51.2 4.7 %collective-permute-done.15.refs_6_ = bf16[592,384]{1,0:T(8,128)(2,1)S(1)} collective-permute-done((bf16[592,384]{1,0:T(8,128)(2,1)S(1)}, bf16[592,384]{1,0:T(8,128)(2,1)S(1)}, u32[]{:S(2)}, u32[]{:S(2)}) %collective-permute-start.15) | collective-permute-done | bytes 454688 | tf_op jit(solution)/shard_map/ppermute | solution.py:552
  55.9 8.8 %collective-permute-done.14.refs_4_ = bf16[592,384]{1,0:T(8,128)(2,1)S(1)} collective-permute-done((bf16[592,384]{1,0:T(8,128)(2,1)S(1)}, bf16[592,384]{1,0:T(8,128)(2,1)S(1)}, u32[]{:S(2)}, u32[]{:S(2)}) %collective-permute-start.14) | collective-permute-done | bytes 454688 | tf_op jit(solution)/shard_map/ppermute | solution.py:552
  68.5 5.8 %shard_map.122 = (bf16[32,48,384]{2,1,0:T(8,128)(2,1)S(1)}, bf16[32,48,384]{2,1,0:T(8,128)(2,1)S(1)}, bf16[32,48,384]{2,1,0:T(8,128)(2,1)S(1)}, f32[16,384]{1,0:...) custom-call(f32[416,384]{1,0:T(8,128)S(1)} %get-tuple-element.108.x_, ...), custom_call_target="tpu_custom_call" | custom-call | flops 1962934272 | bytes 8388608 | tf_op jit(solution)/shard_map/pallas_call | solution.py:525
  75.9 5.1 %shard_map.123 = (f32[416,384]{1,0:T(8,128)S(1)}, f32[16,384]{1,0:T(8,128)S(1)}, bf16[2,2,384,384]{3,2,1,0:T(8,128)(2,1)S(1)}, bf16[2,2,384,384]{3,2,1,0:T(8,128)(2,1)S(1)}) custom-call(bf16[416,384]{1,0:T(8,128)(2,1)S(1)} %bitcast.51, f32[416,384]{1,0:T(8,128)S(1)} %get-tuple-element.113.mid_ref, f32[16,384]{1,0:T(8,128)S(1)} %get-tuple-element.114.vec_ref, ...), custom_call_target="tpu_custom_call" | custom-call | flops 1962934272 | bytes 8388608 | tf_op jit(solution)/shard_map/pallas_call | solution.py:525
  81.1 5.0 %shard_map.124 = (f32[416,384]{1,0:T(8,128)S(1)}, bf16[2,2,208,384]{3,2,1,0:T(8,128)(2,1)S(1)}, bf16[2,2,208,384]{3,2,1,0:T(8,128)(2,1)S(1)}) custom-call(f32[416,384]{1,0:T(8,128)S(1)} %get-tuple-element.125.gm_ref, f32[416,384]{1,0:T(8,128)S(1)} %get-tuple-element.108.x_ref, f32[16,384]{1,0:T(8,128)S(1)} %get-tuple-element.114.vec_ref, ...), custom_call_target="tpu_custom_call" | custom-call | flops 1962934272 | bytes 8388608 | tf_op jit(solution)/shard_map/pallas_call | solution.py:525
  92.4 3.2 %shard_map.128 = f32[1024,384]{1,0:T(8,128)} custom-call(s32[5,1,208]{2,1,0:T(1,128)S(1)} %constant_dynamic-update-slice_fusion.slot_ref, bf16[416,384]{1,0:T(8,128)(2,1)S(1)} %get-tuple-element.141.own_ref, bf16[208,384]{1,0:T(8,128)(2,1)S(1)} %collective-permute-done.23.refs_0_, bf16[208,384]{1,0:T(8,128)(2,1)S(1)} %collective-permute-done.20.refs_1_, ...), custom_call_target="tpu_custom_call" | custom-call | flops 817889280 | bytes 8388608 | tf_op jit(solution)/shard_map/pallas_call | solution.py:525
  95.6 9.9 %shard_map.127 = (bf16[416,384]{1,0:T(8,128)(2,1)S(1)}, bf16[2,2,592,384]{3,2,1,0:T(8,128)(2,1)S(1)}, bf16[2,2,592,384]{3,2,1,0:T(8,128)(2,1)}) custom-call(f32[416,384]{1,0:T(8,128)S(1)} %get-tuple-element.147.g_ref, bf16[416,384]{1,0:T(8,128)(2,1)S(1)} %bitcast.53, f32[416,384]{1,0:T(8,128)S(1)} %get-tuple-element.148.mid_ref, ...), custom_call_target="tpu_custom_call" | custom-call | flops 5888802816 | bytes 8388608 | tf_op jit(solution)/shard_map/pallas_call | solution.py:525
  105.5 6.5 %collective-permute-done.26.refs_2_ = bf16[592,384]{1,0:T(8,128)(2,1)S(1)} collective-permute-done((bf16[592,384]{1,0:T(8,128)(2,1)S(1)}, bf16[592,384]{1,0:T(8,128)(2,1)S(1)}, u32[]{:S(2)}, u32[]{:S(2)}) %collective-permute-start.26) | collective-permute-done | bytes 454688 | tf_op jit(solution)/shard_map/ppermute | solution.py:552
  114.4 3.6 %all-to-all-start = ((bf16[4,160,384]{2,1,0:T(8,128)(2,1)}), bf16[4,160,384]{2,1,0:T(8,128)(2,1)S(1)}, u32[]{:S(2)}, u32[]{:S(2)}) async-start(bf16[4,160,384]{2,1,0:T(8,128)(2,1)} %shard_map.126), calls=%async_computation | async-start | bytes 983040 | tf_op jit(solution)/shard_map/all_to_all | solution.py:889
  118.0 1.9 %add_convert_fusion = (bf16[1,1,592,384]{3,2,1,0:T(8,128)(2,1)S(1)}, bf16[1,1,592,384]{3,2,1,0:T(8,128)(2,1)S(1)}, bf16[1,1,592,384]{3,2,1,0:T(8,128)(2,1)S(1)}, bf16[592,384]{1,0:T(8,128)(2,1)S(1)}) fusion(bf16[2,2,592,384]{3,2,1,0:T(8,128)(2,1)} %collective-permute-done.28, bf16[2,2,592,384]{3,2,1,0:T(8,128)(2,1)S(1)} %get-tuple-element.168), kind=kLoop, calls=%fused_computation | loop fusion | flops 3637248 | bytes 5455872 | tf_op jit(solution)/shard_map/convert_element_type | solution.py:591
  123.0 6.3 %collective-permute-done.30 = bf16[304,384]{1,0:T(8,128)(2,1)S(1)} collective-permute-done((bf16[304,384]{1,0:T(8,128)(2,1)S(1)}, bf16[304,384]{1,0:T(8,128)(2,1)S(1)}, u32[]{:S(2)}, u32[]{:S(2)}) %collective-permute-start.30) | collective-permute-done | bytes 233504 | tf_op jit(solution)/shard_map/ppermute | solution.py:552
  130.3 2.0 %collective-permute-done.32 = bf16[288,384]{1,0:T(8,128)(2,1)S(1)} collective-permute-done((bf16[288,384]{1,0:T(8,128)(2,1)S(1)}, bf16[288,384]{1,0:T(8,128)(2,1)S(1)}, u32[]{:S(2)}, u32[]{:S(2)}) %collective-permute-start.32) | collective-permute-done | bytes 221216 | tf_op jit(solution)/shard_map/ppermute | solution.py:552
  136.9 3.4 %collective-permute-done.33.refs_3_ = bf16[288,384]{1,0:T(8,128)(2,1)S(1)} collective-permute-done((bf16[288,384]{1,0:T(8,128)(2,1)S(1)}, bf16[288,384]{1,0:T(8,128)(2,1)S(1)}, u32[]{:S(2)}, u32[]{:S(2)}) %collective-permute-start.33) | collective-permute-done | bytes 221216 | tf_op jit(solution)/shard_map/ppermute | solution.py:552
  142.1 2.4 %collective-permute-start.39 = (bf16[160,384]{1,0:T(8,128)(2,1)S(1)}, bf16[160,384]{1,0:T(8,128)(2,1)S(1)}, u32[]{:S(2)}, u32[]{:S(2)}) collective-permute-start(bf16[160,384]{1,0:T(8,128)(2,1)S(1)} %get-tuple-element.180), channel_id=1, source_target_pairs={{0,16},{1,17},{2,18},{3,19},{4,20},{5,21},{6,22},{7,23},{8,24},{9,... | collective-permute-start | bytes 368648 | tf_op jit(solution)/shard_map/ppermute | solution.py:552
  146.2 6.8 %collective-permute-done.39.refs_3_ = bf16[160,384]{1,0:T(8,128)(2,1)S(1)} collective-permute-done((bf16[160,384]{1,0:T(8,128)(2,1)S(1)}, bf16[160,384]{1,0:T(8,128)(2,1)S(1)}, u32[]{:S(2)}, u32[]{:S(2)}) %collective-permute-start.39) | collective-permute-done | bytes 122912 | tf_op jit(solution)/shard_map/ppermute | solution.py:552
  (110 shorter events, 40.3 us)
Async XLA Ops:
  2.3 9.6 %collective-permute-start.2 = (bf16[160,384]{1,0:T(8,128)(2,1)}, bf16[160,384]{1,0:T(8,128)(2,1)S(1)}, u32[]{:S(2)}, u32[]{:S(2)}) collective-permute-start(bf16[160,384]{1,0:T(8,128)(2,1)} %get-tuple-element.98.refs_0_), channel_id=1, source_target_pairs={{0,24},{1,25},{2,26},{3,27},{4,28},{5,29},{6,30},{7,31},{8,16},{9,... | collective-permute-start | bytes 368648 | tf_op jit(solution)/shard_map/ppermute | solution.py:552
  7.4 10.6 %collective-permute-start.1 = (bf16[160,384]{1,0:T(8,128)(2,1)}, bf16[160,384]{1,0:T(8,128)(2,1)S(1)}, u32[]{:S(2)}, u32[]{:S(2)}) collective-permute-start(bf16[160,384]{1,0:T(8,128)(2,1)} %get-tuple-element.98.refs_0_), channel_id=1, source_target_pairs={{0,16},{1,17},{2,18},{3,19},{4,20},{5,21},{6,22},{7,23},{8,24},{9,... | collective-permute-start | bytes 368648 | tf_op jit(solution)/shard_map/ppermute | solution.py:552
  7.4 10.6 %collective-permute-start = (bf16[160,384]{1,0:T(8,128)(2,1)}, bf16[160,384]{1,0:T(8,128)(2,1)S(1)}, u32[]{:S(2)}, u32[]{:S(2)}) collective-permute-start(bf16[160,384]{1,0:T(8,128)(2,1)} %get-tuple-element.98.refs_0_), channel_id=1, source_target_pairs={{0,8},{1,9},{2,10},{3,11},{4,12},{5,13},{6,14},{7,15},{8,0},{9,1},... | collective-permute-start | bytes 368648 | tf_op jit(solution)/shard_map/ppermute | solution.py:552
  18.1 17.5 %collective-permute-start.5 = (bf16[592,384]{1,0:T(8,128)(2,1)S(1)}, bf16[592,384]{1,0:T(8,128)(2,1)S(1)}, u32[]{:S(2)}, u32[]{:S(2)}) collective-permute-start(bf16[592,384]{1,0:T(8,128)(2,1)S(1)} %shard_map.119.refs_0_), channel_id=1, source_target_pairs={{0,6},{1,7},{2,4},{3,5},{4,2},{5,3},{6,0},{7,1},{8,14},{9,15},{10,... | collective-permute-start | bytes 1363976 | tf_op jit(solution)/shard_map/ppermute | solution.py:552
  20.6 19.7 %collective-permute-start.4 = (bf16[592,384]{1,0:T(8,128)(2,1)S(1)}, bf16[592,384]{1,0:T(8,128)(2,1)S(1)}, u32[]{:S(2)}, u32[]{:S(2)}) collective-permute-start(bf16[592,384]{1,0:T(8,128)(2,1)S(1)} %shard_map.119.refs_0_), channel_id=1, source_target_pairs={{0,4},{1,5},{2,6},{3,7},{4,0},{5,1},{6,2},{7,3},{8,12},{9,13},{10,... | collective-permute-start | bytes 1363976 | tf_op jit(solution)/shard_map/ppermute | solution.py:552
  21.1 19.3 %collective-permute-start.3 = (bf16[592,384]{1,0:T(8,128)(2,1)S(1)}, bf16[592,384]{1,0:T(8,128)(2,1)S(1)}, u32[]{:S(2)}, u32[]{:S(2)}) collective-permute-start(bf16[592,384]{1,0:T(8,128)(2,1)S(1)} %shard_map.119.refs_0_), channel_id=1, source_target_pairs={{0,2},{1,3},{2,0},{3,1},{4,6},{5,7},{6,4},{7,5},{8,10},{9,11},{10,... | collective-permute-start | bytes 1363976 | tf_op jit(solution)/shard_map/ppermute | solution.py:552
  24.2 9.4 %collective-permute-start.7 = (bf16[160,384]{1,0:T(8,128)(2,1)S(1)}, bf16[160,384]{1,0:T(8,128)(2,1)S(1)}, u32[]{:S(2)}, u32[]{:S(2)}) collective-permute-start(bf16[160,384]{1,0:T(8,128)(2,1)S(1)} %copy-done), channel_id=1, source_target_pairs={{0,16},{1,17},{2,18},{3,19},{4,20},{5,21},{6,22},{7,23},{8,24},{9,... | collective-permute-start | bytes 368648 | tf_op jit(solution)/shard_map/ppermute | solution.py:552
  41.6 14.2 %collective-permute-start.15 = (bf16[592,384]{1,0:T(8,128)(2,1)S(1)}, bf16[592,384]{1,0:T(8,128)(2,1)S(1)}, u32[]{:S(2)}, u32[]{:S(2)}) collective-permute-start(bf16[592,384]{1,0:T(8,128)(2,1)S(1)} %shard_map.120.refs_0_), channel_id=1, source_target_pairs={{0,6},{1,7},{2,4},{3,5},{4,2},{5,3},{6,0},{7,1},{8,14},{9,15},{10,... | collective-permute-start | bytes 1363976 | tf_op jit(solution)/shard_map/ppermute | solution.py:552
  43.3 21.4 %collective-permute-start.14 = (bf16[592,384]{1,0:T(8,128)(2,1)S(1)}, bf16[592,384]{1,0:T(8,128)(2,1)S(1)}, u32[]{:S(2)}, u32[]{:S(2)}) collective-permute-start(bf16[592,384]{1,0:T(8,128)(2,1)S(1)} %shard_map.120.refs_0_), channel_id=1, source_target_pairs={{0,4},{1,5},{2,6},{3,7},{4,0},{5,1},{6,2},{7,3},{8,12},{9,13},{10,... | collective-permute-start | bytes 1363976 | tf_op jit(solution)/shard_map/ppermute | solution.py:552
  44.6 20.1 %collective-permute-start.13 = (bf16[592,384]{1,0:T(8,128)(2,1)S(1)}, bf16[592,384]{1,0:T(8,128)(2,1)S(1)}, u32[]{:S(2)}, u32[]{:S(2)}) collective-permute-start(bf16[592,384]{1,0:T(8,128)(2,1)S(1)} %shard_map.120.refs_0_), channel_id=1, source_target_pairs={{0,2},{1,3},{2,0},{3,1},{4,6},{5,7},{6,4},{7,5},{8,10},{9,11},{10,... | collective-permute-start | bytes 1363976 | tf_op jit(solution)/shard_map/ppermute | solution.py:552
  81.0 7.3 %collective-permute-start.21 = (bf16[2,2,384,384]{3,2,1,0:T(8,128)(2,1)S(1)}, bf16[2,2,384,384]{3,2,1,0:T(8,128)(2,1)S(1)}, u32[]{:S(2)}, u32[]{:S(2)}) collective-permute-start(bf16[2,2,384,384]{3,2,1,0:T(8,128)(2,1)S(1)} %get-tuple-element.134), channel_id=1, source_target_pairs={{0,1},{1,0},{2,3},{3,2},{4,5},{5,4},{6,7},{7,6},{8,9},{9,8},{10,11... | collective-permute-start | bytes 3538952 | tf_op jit(solution)/shard_map/ppermute | solution.py:552
  88.8 16.7 %collective-permute-start.25 = (bf16[592,384]{1,0:T(8,128)(2,1)S(1)}, bf16[592,384]{1,0:T(8,128)(2,1)S(1)}, u32[]{:S(2)}, u32[]{:S(2)}) collective-permute-start(bf16[592,384]{1,0:T(8,128)(2,1)S(1)} %get-tuple-element.144), channel_id=1, source_target_pairs={{0,2},{1,3},{2,0},{3,1},{4,6},{5,7},{6,4},{7,5},{8,10},{9,11},{10,... | collective-permute-start | bytes 1363976 | tf_op jit(solution)/shard_map/ppermute | solution.py:552
  89.9 22.2 %collective-permute-start.26 = (bf16[592,384]{1,0:T(8,128)(2,1)S(1)}, bf16[592,384]{1,0:T(8,128)(2,1)S(1)}, u32[]{:S(2)}, u32[]{:S(2)}) collective-permute-start(bf16[592,384]{1,0:T(8,128)(2,1)S(1)} %get-tuple-element.145), channel_id=1, source_target_pairs={{0,4},{1,5},{2,6},{3,7},{4,0},{5,1},{6,2},{7,3},{8,12},{9,13},{10,... | collective-permute-start | bytes 1363976 | tf_op jit(solution)/shard_map/ppermute | solution.py:552
  90.7 21.3 %collective-permute-start.27 = (bf16[592,384]{1,0:T(8,128)(2,1)S(1)}, bf16[592,384]{1,0:T(8,128)(2,1)S(1)}, u32[]{:S(2)}, u32[]{:S(2)}) collective-permute-start(bf16[592,384]{1,0:T(8,128)(2,1)S(1)} %get-tuple-element.146), channel_id=1, source_target_pairs={{0,6},{1,7},{2,4},{3,5},{4,2},{5,3},{6,0},{7,1},{8,14},{9,15},{10,... | collective-permute-start | bytes 1363976 | tf_op jit(solution)/shard_map/ppermute | solution.py:552
  113.1 20.3 %collective-permute-start.36 = (bf16[208,384]{1,0:T(8,128)(2,1)S(1)}, bf16[208,384]{1,0:T(8,128)(2,1)S(1)}, u32[]{:S(2)}, u32[]{:S(2)}) collective-permute-start(bf16[208,384]{1,0:T(8,128)(2,1)S(1)} %slice.119), channel_id=1, source_target_pairs={{0,2},{1,3},{2,0},{3,1},{4,6},{5,7},{6,4},{7,5},{8,10},{9,11},{10,... | collective-permute-start | bytes 479240 | tf_op jit(solution)/shard_map/ppermute | solution.py:552
  114.2 20.1 %collective-permute-start.35 = (bf16[208,384]{1,0:T(8,128)(2,1)S(1)}, bf16[208,384]{1,0:T(8,128)(2,1)S(1)}, u32[]{:S(2)}, u32[]{:S(2)}) collective-permute-start(bf16[208,384]{1,0:T(8,128)(2,1)S(1)} %slice.119), channel_id=1, source_target_pairs={{0,1},{1,0},{2,3},{3,2},{4,5},{5,4},{6,7},{7,6},{8,9},{9,8},{10,11... | collective-permute-start | bytes 479240 | tf_op jit(solution)/shard_map/ppermute | solution.py:552
  114.4 26.2 %all-to-all-start = ((bf16[4,160,384]{2,1,0:T(8,128)(2,1)}), bf16[4,160,384]{2,1,0:T(8,128)(2,1)S(1)}, u32[]{:S(2)}, u32[]{:S(2)}) async-start(bf16[4,160,384]{2,1,0:T(8,128)(2,1)} %shard_map.126), calls=%async_computation | async-start | bytes 983040 | tf_op jit(solution)/shard_map/all_to_all | solution.py:889
  119.9 17.0 %collective-permute-start.29 = (bf16[288,384]{1,0:T(8,128)(2,1)S(1)}, bf16[288,384]{1,0:T(8,128)(2,1)S(1)}, u32[]{:S(2)}, u32[]{:S(2)}) collective-permute-start(bf16[288,384]{1,0:T(8,128)(2,1)S(1)} %slice_bitcast_fusion.5), channel_id=1, source_target_pairs={{0,2},{1,3},{2,0},{3,1},{4,6},{5,7},{6,4},{7,5},{8,10},{9,11},{10,... | collective-permute-start | bytes 663560 | tf_op jit(solution)/shard_map/ppermute | solution.py:552
  121.0 11.3 %collective-permute-start.32 = (bf16[288,384]{1,0:T(8,128)(2,1)S(1)}, bf16[288,384]{1,0:T(8,128)(2,1)S(1)}, u32[]{:S(2)}, u32[]{:S(2)}) collective-permute-start(bf16[288,384]{1,0:T(8,128)(2,1)S(1)} %slice_bitcast_fusion.3), channel_id=1, source_target_pairs={{0,2},{1,3},{2,0},{3,1},{4,6},{5,7},{6,4},{7,5},{8,10},{9,11},{10,... | collective-permute-start | bytes 663560 | tf_op jit(solution)/shard_map/ppermute | solution.py:552
  122.0 7.2 %collective-permute-start.30 = (bf16[304,384]{1,0:T(8,128)(2,1)S(1)}, bf16[304,384]{1,0:T(8,128)(2,1)S(1)}, u32[]{:S(2)}, u32[]{:S(2)}) collective-permute-start(bf16[304,384]{1,0:T(8,128)(2,1)S(1)} %slice_bitcast_fusion.1), channel_id=1, source_target_pairs={{0,4},{1,5},{2,6},{3,7},{4,0},{5,1},{6,2},{7,3},{8,12},{9,13},{10,... | collective-permute-start | bytes 700424 | tf_op jit(solution)/shard_map/ppermute | solution.py:552
  129.3 7.7 %collective-permute-start.34 = (bf16[304,384]{1,0:T(8,128)(2,1)S(1)}, bf16[304,384]{1,0:T(8,128)(2,1)S(1)}, u32[]{:S(2)}, u32[]{:S(2)}) collective-permute-start(bf16[304,384]{1,0:T(8,128)(2,1)S(1)} %slice_bitcast_fusion), channel_id=1, source_target_pairs={{0,4},{1,5},{2,6},{3,7},{4,0},{5,1},{6,2},{7,3},{8,12},{9,13},{10,... | collective-permute-start | bytes 700424 | tf_op jit(solution)/shard_map/ppermute | solution.py:552
  132.3 8.1 %collective-permute-start.31 = (bf16[304,384]{1,0:T(8,128)(2,1)S(1)}, bf16[304,384]{1,0:T(8,128)(2,1)S(1)}, u32[]{:S(2)}, u32[]{:S(2)}) collective-permute-start(bf16[304,384]{1,0:T(8,128)(2,1)S(1)} %fusion.4), channel_id=1, source_target_pairs={{0,2},{1,3},{2,0},{3,1},{4,6},{5,7},{6,4},{7,5},{8,10},{9,11},{10,... | collective-permute-start | bytes 700424 | tf_op jit(solution)/shard_map/ppermute | solution.py:552
  142.1 10.8 %collective-permute-start.39 = (bf16[160,384]{1,0:T(8,128)(2,1)S(1)}, bf16[160,384]{1,0:T(8,128)(2,1)S(1)}, u32[]{:S(2)}, u32[]{:S(2)}) collective-permute-start(bf16[160,384]{1,0:T(8,128)(2,1)S(1)} %get-tuple-element.180), channel_id=1, source_target_pairs={{0,16},{1,17},{2,18},{3,19},{4,20},{5,21},{6,22},{7,23},{8,24},{9,... | collective-permute-start | bytes 368648 | tf_op jit(solution)/shard_map/ppermute | solution.py:552
  144.5 8.5 %collective-permute-start.40 = (bf16[160,384]{1,0:T(8,128)(2,1)S(1)}, bf16[160,384]{1,0:T(8,128)(2,1)S(1)}, u32[]{:S(2)}, u32[]{:S(2)}) collective-permute-start(bf16[160,384]{1,0:T(8,128)(2,1)S(1)} %get-tuple-element.181), channel_id=1, source_target_pairs={{0,24},{1,25},{2,26},{3,27},{4,28},{5,29},{6,30},{7,31},{8,16},{9,... | collective-permute-start | bytes 368648 | tf_op jit(solution)/shard_map/ppermute | solution.py:552
  (20 other events, 106.5 us)
where the time goes:
time: 154 us
  waiting for transfers between devices  63 us (41%)
  starting transfers between devices  43.4 us (28%)
  Pallas kernels  40.5 us (26%)
  other arithmetic  4.2 us (3%)
  local copies, waits for them, and re-layouts  1.77 us (1%)
    ppermute x41, waiting for transfers between devices, flip(): lax.ppermute(array, ('dp', 'mp'), [(d, d ^ mask) for d in range(devices)])  63 us
    pallas_call x14, Pallas kernels, call(): pl.pallas_call(kernel, out_shape=[jax.ShapeDtypeStruct(shape, dtype) for...  40.5 us
    ppermute x41, starting transfers between devices, flip(): lax.ppermute(array, ('dp', 'mp'), [(d, d ^ mask) for d in range(devices)])  39.8 us
    all_to_all x1, starting transfers between devices, shards(): lax.all_to_all(last_total, ('dp', 'mp'), 0, 0, axis_index_groups=columns,...  3.56 us
  transfers between devices with their start and end apart: 42, of which 21 were waited for; matrix products, arithmetic and copies ran while one was open for 4% of the time, Pallas kernels for 20%

commit v1 on v0

--- a/solution.py
+++ b/solution.py
@@ -891,6 +891,7 @@
             )
         across = flip(grad_first[:rows], 2, devices)
         first_sums = sum_cores(*first_halves, devices)
+        first_sums, across, grad_first = lax.optimization_barrier((first_sums, across, grad_first))
         first_total = sum_plane(plan, first_sums, devices, True)
         beside = flip(grad_first[:rows], 1, devices)
         input_grads = place_grads(grad_first, [beside, across, flip(across, 1, devices)])

time: 154 us -> 158 us (1.026)
  waiting for transfers between devices: 63 us -> 67.9 us
    ppermute x41, waiting for transfers between devices: 63 us -> 67.9 us  [flip(): lax.ppermute(array, ('dp', 'mp'), [(d, d ^ mask) for d in range(devices)])]
  transfers between devices with their start and end apart: 42 -> 42, of which waited for: 21 -> 24; matrix products, arithmetic and copies ran while one was open for 4% -> 3% of each run, Pallas kernels for 20% -> 19%
where the time goes in v1:
time: 158 us; the launch traced here: 157 us
  waiting for transfers between devices  67.9 us (43%)
  starting transfers between devices  43.9 us (28%)
  Pallas kernels  40 us (25%)
  other arithmetic  2.78 us (2%)
  local copies, waits for them, and re-layouts  1.79 us (1%)
    ppermute x41, waiting for transfers between devices, flip(): lax.ppermute(array, ('dp', 'mp'), [(d, d ^ mask) for d in range(devices)])  67.9 us
    ppermute x41, starting transfers between devices, flip(): lax.ppermute(array, ('dp', 'mp'), [(d, d ^ mask) for d in range(devices)])  40.4 us
    pallas_call x14, Pallas kernels, call(): pl.pallas_call(kernel, out_shape=[jax.ShapeDtypeStruct(shape, dtype) for...  40 us
    all_to_all x1, starting transfers between devices, shards(): lax.all_to_all(last_total, ('dp', 'mp'), 0, 0, axis_index_groups=columns,...  3.56 us
  transfers between devices with their start and end apart: 42, of which 24 were waited for; matrix products, arithmetic and copies ran while one was open for 3% of the time, Pallas kernels for 19%

profile of v1, /device:TPU:0, one launch (start us, length us, event | category | flops | bytes accessed | tf_op | source)
XLA Modules:
  0.0 157.4 jit_solution(2799843334568405001)
XLA Ops:
  2.3 5.1 %collective-permute-start.2 = (bf16[160,384]{1,0:T(8,128)(2,1)}, bf16[160,384]{1,0:T(8,128)(2,1)S(1)}, u32[]{:S(2)}, u32[]{:S(2)}) collective-permute-start(bf16[160,384]{1,0:T(8,128)(2,1)} %get-tuple-element.104.refs_0_), channel_id=1, source_target_pairs={{0,24},{1,25},{2,26},{3,27},{4,28},{5,29},{6,30},{7,31},{8,16},{9,... | collective-permute-start | bytes 368648 | tf_op jit(solution)/shard_map/ppermute | solution.py:552
  11.9 6.1 %collective-permute-done.1.refs_2_ = bf16[160,384]{1,0:T(8,128)(2,1)S(1)} collective-permute-done((bf16[160,384]{1,0:T(8,128)(2,1)}, bf16[160,384]{1,0:T(8,128)(2,1)S(1)}, u32[]{:S(2)}, u32[]{:S(2)}) %collective-permute-start.1) | collective-permute-done | bytes 122912 | tf_op jit(solution)/shard_map/ppermute | solution.py:552
  18.1 2.5 %collective-permute-start.5 = (bf16[592,384]{1,0:T(8,128)(2,1)S(1)}, bf16[592,384]{1,0:T(8,128)(2,1)S(1)}, u32[]{:S(2)}, u32[]{:S(2)}) collective-permute-start(bf16[592,384]{1,0:T(8,128)(2,1)S(1)} %shard_map.119.refs_0_), channel_id=1, source_target_pairs={{0,6},{1,7},{2,4},{3,5},{4,2},{5,3},{6,0},{7,1},{8,14},{9,15},{10,... | collective-permute-start | bytes 1363976 | tf_op jit(solution)/shard_map/ppermute | solution.py:552
  21.6 2.5 %collective-permute-start.8 = (bf16[160,384]{1,0:T(8,128)(2,1)S(1)}, bf16[160,384]{1,0:T(8,128)(2,1)S(1)}, u32[]{:S(2)}, u32[]{:S(2)}) collective-permute-start(bf16[160,384]{1,0:T(8,128)(2,1)S(1)} %copy-done), channel_id=1, source_target_pairs={{0,24},{1,25},{2,26},{3,27},{4,28},{5,29},{6,30},{7,31},{8,16},{9,... | collective-permute-start | bytes 368648 | tf_op jit(solution)/shard_map/ppermute | solution.py:552
  24.2 4.2 %collective-permute-done.8.refs_3_ = bf16[160,384]{1,0:T(8,128)(2,1)S(1)} collective-permute-done((bf16[160,384]{1,0:T(8,128)(2,1)S(1)}, bf16[160,384]{1,0:T(8,128)(2,1)S(1)}, u32[]{:S(2)}, u32[]{:S(2)}) %collective-permute-start.8) | collective-permute-done | bytes 122912 | tf_op jit(solution)/shard_map/ppermute | solution.py:552
  28.4 4.3 %collective-permute-start.6 = (bf16[160,384]{1,0:T(8,128)(2,1)S(1)}, bf16[160,384]{1,0:T(8,128)(2,1)S(1)}, u32[]{:S(2)}, u32[]{:S(2)}) collective-permute-start(bf16[160,384]{1,0:T(8,128)(2,1)S(1)} %copy-done), channel_id=1, source_target_pairs={{0,8},{1,9},{2,10},{3,11},{4,12},{5,13},{6,14},{7,15},{8,0},{9,1},... | collective-permute-start | bytes 368648 | tf_op jit(solution)/shard_map/ppermute | solution.py:552
  35.6 4.6 %collective-permute-done.4.refs_4_ = bf16[592,384]{1,0:T(8,128)(2,1)S(1)} collective-permute-done((bf16[592,384]{1,0:T(8,128)(2,1)S(1)}, bf16[592,384]{1,0:T(8,128)(2,1)S(1)}, u32[]{:S(2)}, u32[]{:S(2)}) %collective-permute-start.4) | collective-permute-done | bytes 454688 | tf_op jit(solution)/shard_map/ppermute | solution.py:552
  45.2 6.0 %shard_map.121 = (bf16[32,48,384]{2,1,0:T(8,128)(2,1)S(1)}, bf16[32,48,384]{2,1,0:T(8,128)(2,1)S(1)}, bf16[32,48,384]{2,1,0:T(8,128)(2,1)S(1)}, f32[16,384]{1,0:...) custom-call(bf16[416,384]{1,0:T(8,128)(2,1)S(1)} %bitcast.40, ...), custom_call_target="tpu_custom_call" | custom-call | flops 1962934272 | bytes 8388608 | tf_op jit(solution)/shard_map/pallas_call | solution.py:525
  51.2 4.7 %collective-permute-done.15.refs_6_ = bf16[592,384]{1,0:T(8,128)(2,1)S(1)} collective-permute-done((bf16[592,384]{1,0:T(8,128)(2,1)S(1)}, bf16[592,384]{1,0:T(8,128)(2,1)S(1)}, u32[]{:S(2)}, u32[]{:S(2)}) %collective-permute-start.15) | collective-permute-done | bytes 454688 | tf_op jit(solution)/shard_map/ppermute | solution.py:552
  55.9 8.8 %collective-permute-done.14.refs_4_ = bf16[592,384]{1,0:T(8,128)(2,1)S(1)} collective-permute-done((bf16[592,384]{1,0:T(8,128)(2,1)S(1)}, bf16[592,384]{1,0:T(8,128)(2,1)S(1)}, u32[]{:S(2)}, u32[]{:S(2)}) %collective-permute-start.14) | collective-permute-done | bytes 454688 | tf_op jit(solution)/shard_map/ppermute | solution.py:552
  68.5 5.8 %shard_map.122 = (bf16[32,48,384]{2,1,0:T(8,128)(2,1)S(1)}, bf16[32,48,384]{2,1,0:T(8,128)(2,1)S(1)}, bf16[32,48,384]{2,1,0:T(8,128)(2,1)S(1)}, f32[16,384]{1,0:...) custom-call(f32[416,384]{1,0:T(8,128)S(1)} %get-tuple-element.114.x_, ...), custom_call_target="tpu_custom_call" | custom-call | flops 1962934272 | bytes 8388608 | tf_op jit(solution)/shard_map/pallas_call | solution.py:525
  75.9 5.1 %shard_map.123 = (f32[416,384]{1,0:T(8,128)S(1)}, f32[16,384]{1,0:T(8,128)S(1)}, bf16[2,2,384,384]{3,2,1,0:T(8,128)(2,1)S(1)}, bf16[2,2,384,384]{3,2,1,0:T(8,128)(2,1)S(1)}) custom-call(bf16[416,384]{1,0:T(8,128)(2,1)S(1)} %bitcast.39, f32[416,384]{1,0:T(8,128)S(1)} %get-tuple-element.119.mid_ref, f32[16,384]{1,0:T(8,128)S(1)} %get-tuple-element.120.vec_ref, ...), custom_call_target="tpu_custom_call" | custom-call | flops 1962934272 | bytes 8388608 | tf_op jit(solution)/shard_map/pallas_call | solution.py:525
  81.1 5.0 %shard_map.124 = (f32[416,384]{1,0:T(8,128)S(1)}, bf16[2,2,208,384]{3,2,1,0:T(8,128)(2,1)S(1)}, bf16[2,2,208,384]{3,2,1,0:T(8,128)(2,1)S(1)}) custom-call(f32[416,384]{1,0:T(8,128)S(1)} %get-tuple-element.131.gm_ref, f32[416,384]{1,0:T(8,128)S(1)} %get-tuple-element.114.x_ref, f32[16,384]{1,0:T(8,128)S(1)} %get-tuple-element.120.vec_ref, ...), custom_call_target="tpu_custom_call" | custom-call | flops 1962934272 | bytes 8388608 | tf_op jit(solution)/shard_map/pallas_call | solution.py:525
  92.3 3.2 %shard_map.128 = f32[1024,384]{1,0:T(8,128)} custom-call(s32[5,1,208]{2,1,0:T(1,128)S(1)} %constant_dynamic-update-slice_fusion.slot_ref, bf16[416,384]{1,0:T(8,128)(2,1)S(1)} %get-tuple-element.147.own_ref, bf16[208,384]{1,0:T(8,128)(2,1)S(1)} %collective-permute-done.23.refs_0_, bf16[208,384]{1,0:T(8,128)(2,1)S(1)} %collective-permute-done.20.refs_1_, ...), custom_call_target="tpu_custom_call" | custom-call | flops 817889280 | bytes 8388608 | tf_op jit(solution)/shard_map/pallas_call | solution.py:525
  95.6 9.4 %shard_map.127 = (bf16[416,384]{1,0:T(8,128)(2,1)S(1)}, bf16[2,2,592,384]{3,2,1,0:T(8,128)(2,1)S(1)}, bf16[2,2,592,384]{3,2,1,0:T(8,128)(2,1)S(1)}) custom-call(f32[416,384]{1,0:T(8,128)S(1)} %get-tuple-element.153.g_ref, bf16[416,384]{1,0:T(8,128)(2,1)S(1)} %bitcast.41, f32[416,384]{1,0:T(8,128)S(1)} %get-tuple-element.154.mid_ref, ...), custom_call_target="tpu_custom_call" | custom-call | flops 5888802816 | bytes 8388608 | tf_op jit(solution)/shard_map/pallas_call | solution.py:525
  105.0 7.0 %collective-permute-done.26.refs_2_ = bf16[592,384]{1,0:T(8,128)(2,1)S(1)} collective-permute-done((bf16[592,384]{1,0:T(8,128)(2,1)S(1)}, bf16[592,384]{1,0:T(8,128)(2,1)S(1)}, u32[]{:S(2)}, u32[]{:S(2)}) %collective-permute-start.26) | collective-permute-done | bytes 454688 | tf_op jit(solution)/shard_map/ppermute | solution.py:552
  114.2 2.7 %collective-permute-done.28 = bf16[2,2,592,384]{3,2,1,0:T(8,128)(2,1)S(1)} collective-permute-done((bf16[2,2,592,384]{3,2,1,0:T(8,128)(2,1)S(1)}, bf16[2,2,592,384]{3,2,1,0:T(8,128)(2,1)S(1)}, u32[]{:S(2)}, u32[]{:S(2)}) %collective-permute-start.28) | collective-permute-done | bytes 1818656 | tf_op jit(solution)/shard_map/ppermute | solution.py:552
  117.3 2.4 %collective-permute-done.29.refs_1_ = bf16[208,384]{1,0:T(8,128)(2,1)S(1)} collective-permute-done((bf16[208,384]{1,0:T(8,128)(2,1)S(1)}, bf16[208,384]{1,0:T(8,128)(2,1)S(1)}, u32[]{:S(2)}, u32[]{:S(2)}) %collective-permute-start.29) | collective-permute-done | bytes 159776 | tf_op jit(solution)/shard_map/ppermute | solution.py:552
  120.6 3.6 %all-to-all-start = ((bf16[4,160,384]{2,1,0:T(8,128)(2,1)}), bf16[4,160,384]{2,1,0:T(8,128)(2,1)S(1)}, u32[]{:S(2)}, u32[]{:S(2)}) async-start(bf16[4,160,384]{2,1,0:T(8,128)(2,1)} %shard_map.126), calls=%async_computation | async-start | bytes 983040 | tf_op jit(solution)/shard_map/all_to_all | solution.py:889
  128.8 3.8 %collective-permute-done.33 = bf16[288,384]{1,0:T(8,128)(2,1)S(1)} collective-permute-done((bf16[288,384]{1,0:T(8,128)(2,1)S(1)}, bf16[288,384]{1,0:T(8,128)(2,1)S(1)}, u32[]{:S(2)}, u32[]{:S(2)}) %collective-permute-start.33) | collective-permute-done | bytes 221216 | tf_op jit(solution)/shard_map/ppermute | solution.py:552
  139.4 2.6 %collective-permute-done.32.refs_2_ = bf16[304,384]{1,0:T(8,128)(2,1)S(1)} collective-permute-done((bf16[304,384]{1,0:T(8,128)(2,1)S(1)}, bf16[304,384]{1,0:T(8,128)(2,1)S(1)}, u32[]{:S(2)}, u32[]{:S(2)}) %collective-permute-start.32) | collective-permute-done | bytes 233504 | tf_op jit(solution)/shard_map/ppermute | solution.py:552
  142.3 2.1 %collective-permute-start.38 = (bf16[160,384]{1,0:T(8,128)(2,1)S(1)}, bf16[160,384]{1,0:T(8,128)(2,1)S(1)}, u32[]{:S(2)}, u32[]{:S(2)}) collective-permute-start(bf16[160,384]{1,0:T(8,128)(2,1)S(1)} %get-tuple-element.191), channel_id=1, source_target_pairs={{0,8},{1,9},{2,10},{3,11},{4,12},{5,13},{6,14},{7,15},{8,0},{9,1},... | collective-permute-start | bytes 368648 | tf_op jit(solution)/shard_map/ppermute | solution.py:552
  144.4 2.4 %collective-permute-start.39 = (bf16[160,384]{1,0:T(8,128)(2,1)S(1)}, bf16[160,384]{1,0:T(8,128)(2,1)S(1)}, u32[]{:S(2)}, u32[]{:S(2)}) collective-permute-start(bf16[160,384]{1,0:T(8,128)(2,1)S(1)} %get-tuple-element.192), channel_id=1, source_target_pairs={{0,16},{1,17},{2,18},{3,19},{4,20},{5,21},{6,22},{7,23},{8,24},{9,... | collective-permute-start | bytes 368648 | tf_op jit(solution)/shard_map/ppermute | solution.py:552
  148.8 7.8 %collective-permute-done.39.refs_3_ = bf16[160,384]{1,0:T(8,128)(2,1)S(1)} collective-permute-done((bf16[160,384]{1,0:T(8,128)(2,1)S(1)}, bf16[160,384]{1,0:T(8,128)(2,1)S(1)}, u32[]{:S(2)}, u32[]{:S(2)}) %collective-permute-start.39) | collective-permute-done | bytes 122912 | tf_op jit(solution)/shard_map/ppermute | solution.py:552
  (111 shorter events, 45.0 us)
Async XLA Ops:
  2.3 9.6 %collective-permute-start.2 = (bf16[160,384]{1,0:T(8,128)(2,1)}, bf16[160,384]{1,0:T(8,128)(2,1)S(1)}, u32[]{:S(2)}, u32[]{:S(2)}) collective-permute-start(bf16[160,384]{1,0:T(8,128)(2,1)} %get-tuple-element.104.refs_0_), channel_id=1, source_target_pairs={{0,24},{1,25},{2,26},{3,27},{4,28},{5,29},{6,30},{7,31},{8,16},{9,... | collective-permute-start | bytes 368648 | tf_op jit(solution)/shard_map/ppermute | solution.py:552
  7.4 10.6 %collective-permute-start.1 = (bf16[160,384]{1,0:T(8,128)(2,1)}, bf16[160,384]{1,0:T(8,128)(2,1)S(1)}, u32[]{:S(2)}, u32[]{:S(2)}) collective-permute-start(bf16[160,384]{1,0:T(8,128)(2,1)} %get-tuple-element.104.refs_0_), channel_id=1, source_target_pairs={{0,16},{1,17},{2,18},{3,19},{4,20},{5,21},{6,22},{7,23},{8,24},{9,... | collective-permute-start | bytes 368648 | tf_op jit(solution)/shard_map/ppermute | solution.py:552
  7.4 10.6 %collective-permute-start = (bf16[160,384]{1,0:T(8,128)(2,1)}, bf16[160,384]{1,0:T(8,128)(2,1)S(1)}, u32[]{:S(2)}, u32[]{:S(2)}) collective-permute-start(bf16[160,384]{1,0:T(8,128)(2,1)} %get-tuple-element.104.refs_0_), channel_id=1, source_target_pairs={{0,8},{1,9},{2,10},{3,11},{4,12},{5,13},{6,14},{7,15},{8,0},{9,1},... | collective-permute-start | bytes 368648 | tf_op jit(solution)/shard_map/ppermute | solution.py:552
  18.1 17.5 %collective-permute-start.5 = (bf16[592,384]{1,0:T(8,128)(2,1)S(1)}, bf16[592,384]{1,0:T(8,128)(2,1)S(1)}, u32[]{:S(2)}, u32[]{:S(2)}) collective-permute-start(bf16[592,384]{1,0:T(8,128)(2,1)S(1)} %shard_map.119.refs_0_), channel_id=1, source_target_pairs={{0,6},{1,7},{2,4},{3,5},{4,2},{5,3},{6,0},{7,1},{8,14},{9,15},{10,... | collective-permute-start | bytes 1363976 | tf_op jit(solution)/shard_map/ppermute | solution.py:552
  20.6 19.7 %collective-permute-start.4 = (bf16[592,384]{1,0:T(8,128)(2,1)S(1)}, bf16[592,384]{1,0:T(8,128)(2,1)S(1)}, u32[]{:S(2)}, u32[]{:S(2)}) collective-permute-start(bf16[592,384]{1,0:T(8,128)(2,1)S(1)} %shard_map.119.refs_0_), channel_id=1, source_target_pairs={{0,4},{1,5},{2,6},{3,7},{4,0},{5,1},{6,2},{7,3},{8,12},{9,13},{10,... | collective-permute-start | bytes 1363976 | tf_op jit(solution)/shard_map/ppermute | solution.py:552
  21.1 19.3 %collective-permute-start.3 = (bf16[592,384]{1,0:T(8,128)(2,1)S(1)}, bf16[592,384]{1,0:T(8,128)(2,1)S(1)}, u32[]{:S(2)}, u32[]{:S(2)}) collective-permute-start(bf16[592,384]{1,0:T(8,128)(2,1)S(1)} %shard_map.119.refs_0_), channel_id=1, source_target_pairs={{0,2},{1,3},{2,0},{3,1},{4,6},{5,7},{6,4},{7,5},{8,10},{9,11},{10,... | collective-permute-start | bytes 1363976 | tf_op jit(solution)/shard_map/ppermute | solution.py:552
  24.2 9.4 %collective-permute-start.7 = (bf16[160,384]{1,0:T(8,128)(2,1)S(1)}, bf16[160,384]{1,0:T(8,128)(2,1)S(1)}, u32[]{:S(2)}, u32[]{:S(2)}) collective-permute-start(bf16[160,384]{1,0:T(8,128)(2,1)S(1)} %copy-done), channel_id=1, source_target_pairs={{0,16},{1,17},{2,18},{3,19},{4,20},{5,21},{6,22},{7,23},{8,24},{9,... | collective-permute-start | bytes 368648 | tf_op jit(solution)/shard_map/ppermute | solution.py:552
  28.4 7.2 %collective-permute-start.6 = (bf16[160,384]{1,0:T(8,128)(2,1)S(1)}, bf16[160,384]{1,0:T(8,128)(2,1)S(1)}, u32[]{:S(2)}, u32[]{:S(2)}) collective-permute-start(bf16[160,384]{1,0:T(8,128)(2,1)S(1)} %copy-done), channel_id=1, source_target_pairs={{0,8},{1,9},{2,10},{3,11},{4,12},{5,13},{6,14},{7,15},{8,0},{9,1},... | collective-permute-start | bytes 368648 | tf_op jit(solution)/shard_map/ppermute | solution.py:552
  41.6 14.2 %collective-permute-start.15 = (bf16[592,384]{1,0:T(8,128)(2,1)S(1)}, bf16[592,384]{1,0:T(8,128)(2,1)S(1)}, u32[]{:S(2)}, u32[]{:S(2)}) collective-permute-start(bf16[592,384]{1,0:T(8,128)(2,1)S(1)} %shard_map.120.refs_0_), channel_id=1, source_target_pairs={{0,6},{1,7},{2,4},{3,5},{4,2},{5,3},{6,0},{7,1},{8,14},{9,15},{10,... | collective-permute-start | bytes 1363976 | tf_op jit(solution)/shard_map/ppermute | solution.py:552
  43.3 21.4 %collective-permute-start.14 = (bf16[592,384]{1,0:T(8,128)(2,1)S(1)}, bf16[592,384]{1,0:T(8,128)(2,1)S(1)}, u32[]{:S(2)}, u32[]{:S(2)}) collective-permute-start(bf16[592,384]{1,0:T(8,128)(2,1)S(1)} %shard_map.120.refs_0_), channel_id=1, source_target_pairs={{0,4},{1,5},{2,6},{3,7},{4,0},{5,1},{6,2},{7,3},{8,12},{9,13},{10,... | collective-permute-start | bytes 1363976 | tf_op jit(solution)/shard_map/ppermute | solution.py:552
  44.6 20.1 %collective-permute-start.13 = (bf16[592,384]{1,0:T(8,128)(2,1)S(1)}, bf16[592,384]{1,0:T(8,128)(2,1)S(1)}, u32[]{:S(2)}, u32[]{:S(2)}) collective-permute-start(bf16[592,384]{1,0:T(8,128)(2,1)S(1)} %shard_map.120.refs_0_), channel_id=1, source_target_pairs={{0,2},{1,3},{2,0},{3,1},{4,6},{5,7},{6,4},{7,5},{8,10},{9,11},{10,... | collective-permute-start | bytes 1363976 | tf_op jit(solution)/shard_map/ppermute | solution.py:552
  81.0 7.3 %collective-permute-start.21 = (bf16[2,2,384,384]{3,2,1,0:T(8,128)(2,1)S(1)}, bf16[2,2,384,384]{3,2,1,0:T(8,128)(2,1)S(1)}, u32[]{:S(2)}, u32[]{:S(2)}) collective-permute-start(bf16[2,2,384,384]{3,2,1,0:T(8,128)(2,1)S(1)} %get-tuple-element.140), channel_id=1, source_target_pairs={{0,1},{1,0},{2,3},{3,2},{4,5},{5,4},{6,7},{7,6},{8,9},{9,8},{10,11... | collective-permute-start | bytes 3538952 | tf_op jit(solution)/shard_map/ppermute | solution.py:552
  88.8 16.2 %collective-permute-start.25 = (bf16[592,384]{1,0:T(8,128)(2,1)S(1)}, bf16[592,384]{1,0:T(8,128)(2,1)S(1)}, u32[]{:S(2)}, u32[]{:S(2)}) collective-permute-start(bf16[592,384]{1,0:T(8,128)(2,1)S(1)} %get-tuple-element.150), channel_id=1, source_target_pairs={{0,2},{1,3},{2,0},{3,1},{4,6},{5,7},{6,4},{7,5},{8,10},{9,11},{10,... | collective-permute-start | bytes 1363976 | tf_op jit(solution)/shard_map/ppermute | solution.py:552
  89.9 22.2 %collective-permute-start.26 = (bf16[592,384]{1,0:T(8,128)(2,1)S(1)}, bf16[592,384]{1,0:T(8,128)(2,1)S(1)}, u32[]{:S(2)}, u32[]{:S(2)}) collective-permute-start(bf16[592,384]{1,0:T(8,128)(2,1)S(1)} %get-tuple-element.151), channel_id=1, source_target_pairs={{0,4},{1,5},{2,6},{3,7},{4,0},{5,1},{6,2},{7,3},{8,12},{9,13},{10,... | collective-permute-start | bytes 1363976 | tf_op jit(solution)/shard_map/ppermute | solution.py:552
  90.7 21.3 %collective-permute-start.27 = (bf16[592,384]{1,0:T(8,128)(2,1)S(1)}, bf16[592,384]{1,0:T(8,128)(2,1)S(1)}, u32[]{:S(2)}, u32[]{:S(2)}) collective-permute-start(bf16[592,384]{1,0:T(8,128)(2,1)S(1)} %get-tuple-element.152), channel_id=1, source_target_pairs={{0,6},{1,7},{2,4},{3,5},{4,2},{5,3},{6,0},{7,1},{8,14},{9,15},{10,... | collective-permute-start | bytes 1363976 | tf_op jit(solution)/shard_map/ppermute | solution.py:552
  119.7 8.0 %collective-permute-start.31 = (bf16[304,384]{1,0:T(8,128)(2,1)S(1)}, bf16[304,384]{1,0:T(8,128)(2,1)S(1)}, u32[]{:S(2)}, u32[]{:S(2)}) collective-permute-start(bf16[304,384]{1,0:T(8,128)(2,1)S(1)} %slice.100), channel_id=1, source_target_pairs={{0,4},{1,5},{2,6},{3,7},{4,0},{5,1},{6,2},{7,3},{8,12},{9,13},{10,... | collective-permute-start | bytes 700424 | tf_op jit(solution)/shard_map/ppermute | solution.py:552
  120.6 21.6 %all-to-all-start = ((bf16[4,160,384]{2,1,0:T(8,128)(2,1)}), bf16[4,160,384]{2,1,0:T(8,128)(2,1)S(1)}, u32[]{:S(2)}, u32[]{:S(2)}) async-start(bf16[4,160,384]{2,1,0:T(8,128)(2,1)} %shard_map.126), calls=%async_computation | async-start | bytes 983040 | tf_op jit(solution)/shard_map/all_to_all | solution.py:889
  124.2 9.7 %collective-permute-start.36 = (bf16[208,384]{1,0:T(8,128)(2,1)S(1)}, bf16[208,384]{1,0:T(8,128)(2,1)S(1)}, u32[]{:S(2)}, u32[]{:S(2)}) collective-permute-start(bf16[208,384]{1,0:T(8,128)(2,1)S(1)} %slice.104), channel_id=1, source_target_pairs={{0,1},{1,0},{2,3},{3,2},{4,5},{5,4},{6,7},{7,6},{8,9},{9,8},{10,11... | collective-permute-start | bytes 479240 | tf_op jit(solution)/shard_map/ppermute | solution.py:552
  124.4 8.3 %collective-permute-start.33 = (bf16[288,384]{1,0:T(8,128)(2,1)S(1)}, bf16[288,384]{1,0:T(8,128)(2,1)S(1)}, u32[]{:S(2)}, u32[]{:S(2)}) collective-permute-start(bf16[288,384]{1,0:T(8,128)(2,1)S(1)} %slice.102), channel_id=1, source_target_pairs={{0,2},{1,3},{2,0},{3,1},{4,6},{5,7},{6,4},{7,5},{8,10},{9,11},{10,... | collective-permute-start | bytes 663560 | tf_op jit(solution)/shard_map/ppermute | solution.py:552
  125.5 11.8 %collective-permute-start.30 = (bf16[288,384]{1,0:T(8,128)(2,1)S(1)}, bf16[288,384]{1,0:T(8,128)(2,1)S(1)}, u32[]{:S(2)}, u32[]{:S(2)}) collective-permute-start(bf16[288,384]{1,0:T(8,128)(2,1)S(1)} %slice.98), channel_id=1, source_target_pairs={{0,2},{1,3},{2,0},{3,1},{4,6},{5,7},{6,4},{7,5},{8,10},{9,11},{10,... | collective-permute-start | bytes 663560 | tf_op jit(solution)/shard_map/ppermute | solution.py:552
  126.5 10.8 %collective-permute-start.35 = (bf16[304,384]{1,0:T(8,128)(2,1)S(1)}, bf16[304,384]{1,0:T(8,128)(2,1)S(1)}, u32[]{:S(2)}, u32[]{:S(2)}) collective-permute-start(bf16[304,384]{1,0:T(8,128)(2,1)S(1)} %slice.103), channel_id=1, source_target_pairs={{0,4},{1,5},{2,6},{3,7},{4,0},{5,1},{6,2},{7,3},{8,12},{9,13},{10,... | collective-permute-start | bytes 700424 | tf_op jit(solution)/shard_map/ppermute | solution.py:552
  127.8 14.2 %collective-permute-start.32 = (bf16[304,384]{1,0:T(8,128)(2,1)S(1)}, bf16[304,384]{1,0:T(8,128)(2,1)S(1)}, u32[]{:S(2)}, u32[]{:S(2)}) collective-permute-start(bf16[304,384]{1,0:T(8,128)(2,1)S(1)} %add_convert_fusion.4), channel_id=1, source_target_pairs={{0,2},{1,3},{2,0},{3,1},{4,6},{5,7},{6,4},{7,5},{8,10},{9,11},{10,... | collective-permute-start | bytes 700424 | tf_op jit(solution)/shard_map/ppermute | solution.py:552
  144.4 12.2 %collective-permute-start.39 = (bf16[160,384]{1,0:T(8,128)(2,1)S(1)}, bf16[160,384]{1,0:T(8,128)(2,1)S(1)}, u32[]{:S(2)}, u32[]{:S(2)}) collective-permute-start(bf16[160,384]{1,0:T(8,128)(2,1)S(1)} %get-tuple-element.192), channel_id=1, source_target_pairs={{0,16},{1,17},{2,18},{3,19},{4,20},{5,21},{6,22},{7,23},{8,24},{9,... | collective-permute-start | bytes 368648 | tf_op jit(solution)/shard_map/ppermute | solution.py:552
  146.7 9.8 %collective-permute-start.40 = (bf16[160,384]{1,0:T(8,128)(2,1)S(1)}, bf16[160,384]{1,0:T(8,128)(2,1)S(1)}, u32[]{:S(2)}, u32[]{:S(2)}) collective-permute-start(bf16[160,384]{1,0:T(8,128)(2,1)S(1)} %get-tuple-element.193), channel_id=1, source_target_pairs={{0,24},{1,25},{2,26},{3,27},{4,28},{5,29},{6,30},{7,31},{8,16},{9,... | collective-permute-start | bytes 368648 | tf_op jit(solution)/shard_map/ppermute | solution.py:552
  (20 other events, 105.4 us)
